TPU v7x, 128 devices: a whole 4x4x4 slice. The times are simulated.
128 devices in a mesh: role: 8 (over z, core), dev: 16 (over y, x).
Axes of the slice: x: 4, y: 4, z: 4, core: 2. Of those that a mesh axis runs over, the one named last changes fastest.
Arguments:
- hidden_rows: bfloat16 [16384, 21504], P(('role', 'dev')), may hold values from -6 to 6
- lengths: int32 [128, 4], P(('role', 'dev')), may hold values from 1 to 32, as said below
- balance: int32 [4096, 1], P(('role', 'dev')), may hold values from 0 to 7; in each aligned block of 32 rows (0 to 31, 32 to 63, ...) at most 5 rows name the same one
- cotangent: bfloat16 [20480, 3584], P(('role', 'dev')), may hold values from -0.046875 to 0.046875
Outputs:
- grad_weight: float32 [3584, 21504], P('role', 'dev')
Inputs may be any that keep to these rules, and one draw needn't show every extreme that they name: `lengths`: on every device one slot has length exactly 32. `balance`: the 32 blocks of one device send at most 5 blocks to one draft group; in every draw some device sends exactly 5 blocks to one group.
All inputs are finite; a program needn't handle non-finite values.
Results may differ from a plain program's by a relative error of at most 0.0003.
Values may be sent and summed in bfloat16 or wider, within the bound.
No kernel may reach another device: no remote copies, remote signals or barrier semaphores. Data moves between devices by JAX's collectives and lax.ppermute only.
A program may use at most 192 MiB of HBM per device.

v0:
```python
import jax
import jax.numpy as jnp
from jax import lax
from jax.sharding import PartitionSpec as P


def body(hidden_rows, lengths, balance, cotangent):
    role_count = lax.axis_size("role")
    dev_count = lax.axis_size("dev")
    tok_count, width_in = hidden_rows.shape
    seq_count = lengths.shape[1]
    slot_len = tok_count // seq_count
    block_count = balance.shape[0]
    block_rows = tok_count // block_count
    pair_rows = cotangent.shape[0] // role_count
    capacity = pair_rows // block_rows
    slice_width = width_in // dev_count
    positions = lax.broadcasted_iota(jnp.int32, (seq_count, slot_len), 1)
    keeping = (positions < lengths[0][:, None]).reshape(tok_count, 1)
    masked = jnp.where(keeping, hidden_rows, jnp.zeros_like(hidden_rows))
    groups = balance[:, 0]
    onehot = (
        groups[:, None] == lax.broadcasted_iota(jnp.int32, (block_count, role_count), 1)
    ).astype(jnp.int32)
    earlier = jnp.cumsum(onehot, axis=0) - onehot
    block_rank = jnp.sum(earlier * onehot, axis=1)
    slot_index = groups * capacity + block_rank
    placing = (
        slot_index[:, None]
        == lax.broadcasted_iota(jnp.int32, (block_count, role_count * capacity), 1)
    ).astype(jnp.bfloat16)
    packed = lax.dot_general(
        placing,
        masked.reshape(block_count, block_rows * width_in),
        (((0,), (0,)), ((), ())),
        preferred_element_type=jnp.float32,
    ).astype(jnp.bfloat16)
    outgoing = packed.reshape(role_count, pair_rows, width_in)
    spread = (
        outgoing.reshape(role_count, pair_rows, dev_count, slice_width)
        .transpose(0, 2, 1, 3)
        .reshape(role_count * dev_count, pair_rows, slice_width)
    )
    arrived = lax.all_to_all(spread, ("role", "dev"), split_axis=0, concat_axis=0, tiled=True)
    arrived = arrived.reshape(role_count, dev_count, pair_rows, slice_width).transpose(1, 0, 2, 3)
    features = arrived.reshape(-1, slice_width)
    every_cot = lax.all_gather(cotangent, "dev", axis=0, tiled=True)
    return lax.psum_scatter(
        lax.dot_general(
            every_cot, features, (((0,), (0,)), ((), ())), preferred_element_type=jnp.float32
        ),
        "role",
        scatter_dimension=0,
        tiled=True,
    )


def solution(mesh):
    in_specs = (
        P(("role", "dev"), None),
        P(("role", "dev"), None),
        P(("role", "dev"), None),
        P(("role", "dev"), None),
    )
    out_specs = P("role", "dev")
    return jax.shard_map(body, mesh=mesh, in_specs=in_specs, out_specs=out_specs, check_vma=False)
```

profile of v0, /device:TPU:1, one launch (start us, length us, event | category | flops | bytes accessed | tf_op | source)
XLA Modules:
  0.0 412.1 jit_solution(17163207941703207488)
XLA Ops:
  6.5 0.0 all-gather.2.cloned.1.call-start
  6.5 0.7 all-gather.2.cloned.1.call-update
  7.3 0.0 reduce-scatter.4.cloned.1.call-start
  7.3 0.7 iota_compare_fusion.3
  8.0 0.1 lt.20
  8.1 5.4 %broadcast_select_fusion = bf16[128,21504]{1,0:T(8,128)(2,1)} fusion(bf16[128,21504]{1,0:T(8,128)(2,1)} %param.4, pred[128]{0:T(512)(128)(4,1)S(1)} %lt.20), kind=kLoop, calls=%fused_computation.3 | loop fusion | flops 2752512 | bytes 11010176 | tf_op jit(solution)/shard_map/jit(_where)/select_n | solution.py:20
  13.5 0.0 copy-start
  13.5 7.6 %reshape.29 = bf16[32,86016]{1,0:T(8,128)(2,1)} reshape(bf16[128,21504]{1,0:T(8,128)(2,1)} %broadcast_select_fusion) | data formatting | bytes 11010048 | tf_op jit(solution)/shard_map/reshape | solution.py:34
  21.1 0.0 copy-done
  21.1 0.1 fusion
  21.2 0.1 reduce_window_sum.11
  21.2 0.2 select_reduce_fusion
  21.4 8.2 %convolution_convert_fusion = bf16[40,86016]{1,0:T(8,128)(2,1)} fusion(bf16[32,86016]{1,0:T(8,128)(2,1)} %reshape.29, s32[32]{0:T(128)S(1)} %fusion.2), kind=kOutput, calls=%fused_computation | convolution fusion | flops 223642880 | bytes 12386432 | tf_op jit(solution)/shard_map/dot_general | solution.py:32
  29.6 11.4 %reshape_reshape.3 = bf16[8,20,16,1344]{3,2,1,0:T(8,128)(2,1)} reshape(bf16[40,86016]{1,0:T(8,128)(2,1)} %convolution_convert_fusion) | data formatting | bytes 13762560 | tf_op jit(solution)/shard_map/reshape;reshape | solution.py:40
  41.0 4.0 copy.9
  45.0 7.6 %copy.10 = bf16[128,20,1344]{2,1,0:T(8,128)(2,1)} copy(bf16[128,20,1344]{2,0,1:T(8,128)(2,1)S(1)} %bitcast.23) | data formatting | bytes 13762560 | tf_op jit(solution)/shard_map/reshape | solution.py:42
  52.5 177.2 %all_to_all.5 = bf16[128,20,1344]{2,1,0:T(8,128)(2,1)} all-to-all(bf16[128,20,1344]{2,1,0:T(8,128)(2,1)} %copy.10), channel_id=1, replica_groups=mesh['role'=8,'dev'=16] {'role','dev'}, dimensions={0} | all-to-all | bytes 13762560 | tf_op jit(solution)/shard_map/all_to_all | solution.py:44
  229.7 8.0 %copy.16 = bf16[8,16,20,1344]{3,2,0,1:T(8,128)(2,1)} copy(bf16[8,16,20,1344]{3,2,1,0:T(8,128)(2,1)} %bitcast.21) | data formatting | bytes 13762560 | tf_op jit(solution)/shard_map/reshape | solution.py:45
  237.7 12.0 %reshape.32 = bf16[2560,1344]{1,0:T(8,128)(2,1)} reshape(bf16[16,8,20,1344]{3,2,1,0:T(8,128)(2,1)} %bitcast.22) | data formatting | bytes 13762560 | tf_op jit(solution)/shard_map/reshape | solution.py:46
  249.7 0.0 all-gather.2.cloned.1.call-done
  249.7 32.0 %convolution_bitcast_fusion = f32[3584,1344]{0,1:T(8,128)} fusion(bf16[2560,1344]{1,0:T(8,128)(2,1)} %reshape.32, bf16[2560,3584]{1,0:T(8,128)(2,1)} %all-gather.2.cloned.1.call-done), kind=kOutput, calls=%fused_computation.1 | convolution fusion | flops 24662507520 | bytes 44498944 | tf_op jit(solution)/shard_map/dot_general | solution.py:49
  281.6 20.3 %copy.13 = f32[3584,1344]{1,0:T(8,128)} copy(f32[3584,1344]{0,1:T(8,128)} %convolution_bitcast_fusion) | data formatting | bytes 38535168
  301.9 0.0 reduce-scatter.4.cloned.1.call-update
  301.9 103.3 %reduce-scatter.4.cloned.1.call-done = f32[448,1344]{1,0:T(8,128)} async-done(((f32[3584,1344]{1,0:T(8,128)}), f32[448,1344]{1,0:T(8,128)}) %reduce-scatter.4.cloned.1.call-update) | async-done | bytes 2408464 | tf_op jit(solution)/shard_map/reduce_scatter | solution.py:48
  (1 shorter events, 0.0 us)
Async XLA Ops:
  6.5 243.1 %all-gather.2.cloned.1.call-start = ((), (), s32[]{:S(2)}) async-start(), calls=%async_computation.2 | async-start | bytes 19496960 | tf_op jit(solution)/shard_map/all_gather | solution.py:47
  7.3 398.0 %reduce-scatter.4.cloned.1.call-start = ((), (), s32[]{:S(2)}) async-start(), calls=%async_computation.3 | async-start | bytes 22708224 | tf_op jit(solution)/shard_map/reduce_scatter | solution.py:48
  13.5 7.6 %copy-start = (s32[32,1]{0,1:T(1,128)S(1)}, s32[32,1]{0,1:T(1,128)}, u32[]{:S(2)}) copy-start(s32[32,1]{0,1:T(1,128)} %param.6) | copy-start | bytes 388
Sparse Core Ops, SparseCore 0:
  9.5 214.2 all-gather.1
  302.0 103.1 reduce-scatter.3
where the time goes:
time: 413 us; the launch traced here: 412 us
  blocking collectives  177 us (43%)
  waiting for transfers between devices  104 us (25%)
  local copies, waits for them, and re-layouts  70.9 us (17%)
  matrix products  40.1 us (10%)
  between operations  13.4 us (3%)
  other arithmetic  6.41 us (2%)
    all_to_all x1, blocking collectives, body(): lax.all_to_all(spread, ('role', 'dev'), split_axis=0, concat_axis=0, tile...  177 us
    reduce_scatter x1, waiting for transfers between devices, body(): lax.psum_scatter(lax.dot_general(every_cot, features, (((0,), (0,)), ((),...  103 us
    dot_general x1, matrix products, body(): lax.dot_general(every_cot, features, (((0,), (0,)), ((), ())), preferred_...  32 us
    unnamed x3, local copies, waits for them, and re-layouts  20.3 us
    another operation x2, local copies, waits for them, and re-layouts, body(): outgoing.reshape(role_count, pair_rows, dev_count, slice_width)  15.3 us
    reshape x1, local copies, waits for them, and re-layouts, body(): features = arrived.reshape(-1, slice_width)  12 us
  transfers between devices with their start and end apart: 2, of which 1 were waited for; matrix products, arithmetic and copies ran while one was open for 16% of the time, Pallas kernels for 0%

commit v1 on v0

v1 whole, which is shorter than its diff:
```python
import functools

import jax
import jax.numpy as jnp
from jax import lax
from jax.experimental import pallas as pl
from jax.experimental.pallas import tpu as pltpu
from jax.sharding import PartitionSpec as P

PARTS = 4
FIRST_COLS = 384


def windows(hidden_rows, starts, width):
    tok_count = hidden_rows.shape[0]
    dev_count = len(starts)
    step = starts[2] - starts[0]
    first, second = starts[0], starts[1] - starts[0]

    def kernel(rows_ref, out_ref):
        out_ref[0] = rows_ref[...]

    def where(i):
        return 0, pl.multiple_of(first + (i // 2) * step + (i % 2) * second, 128)

    return pl.pallas_call(
        kernel,
        grid=(dev_count,),
        in_specs=[pl.BlockSpec((pl.Element(tok_count), pl.Element(width)), where)],
        out_specs=pl.BlockSpec((1, tok_count, width), lambda i: (i, 0, 0)),
        out_shape=jax.ShapeDtypeStruct((dev_count, tok_count, width), hidden_rows.dtype),
        name="cut_windows",
    )(hidden_rows)


def sort_blocks(cotangent, targets, role_count):
    rows, width = cotangent.shape
    block = rows // role_count
    cols = width // 4

    def kernel(targets_ref, cot_ref, *out_refs):
        for j in range(role_count):
            row = lax.broadcasted_iota(jnp.int32, (block, rows), 0)
            column = lax.broadcasted_iota(jnp.int32, (block, rows), 1)
            taking = (column == row + targets_ref[j] * block).astype(jnp.bfloat16)
            out_refs[j][...] = jnp.dot(
                taking, cot_ref[...], preferred_element_type=jnp.float32
            ).astype(jnp.bfloat16)

    return pl.pallas_call(
        kernel,
        grid=(4,),
        in_specs=[
            pl.BlockSpec(memory_space=pltpu.SMEM),
            pl.BlockSpec((rows, cols), lambda i: (0, i)),
        ],
        out_specs=[pl.BlockSpec((block, cols), lambda i: (0, i))] * role_count,
        out_shape=[jax.ShapeDtypeStruct((block, width), cotangent.dtype)] * role_count,
        name="sort_blocks",
    )(targets, cotangent)


def pair_rows(blocks, places, role_count, parts):
    block, width = blocks[0].shape
    count = len(blocks)
    tok_count = places.shape[2]
    share = width // role_count
    piece = share // parts
    fold = 2

    def kernel(places_ref, *refs):
        ins, outs = refs[:count], refs[count:]
        total = jnp.zeros((fold * share, tok_count), jnp.float32)
        for j in range(count):
            total += lax.dot_general(
                ins[j][...],
                places_ref[j],
                (((0,), (0,)), ((), ())),
                preferred_element_type=jnp.float32,
            )
        total = total.astype(jnp.bfloat16)
        for p in range(parts):
            for q in range(fold):
                at = q * share + p * piece
                outs[p][q * piece : (q + 1) * piece] = total[at : at + piece]

    return pl.pallas_call(
        kernel,
        grid=(role_count // fold,),
        in_specs=[pl.BlockSpec((count, block, tok_count), lambda i: (0, 0, 0))]
        + [pl.BlockSpec((block, fold * share), lambda i: (0, i))] * count,
        out_specs=[pl.BlockSpec((fold * piece, tok_count), lambda i: (i, 0))] * parts,
        out_shape=[jax.ShapeDtypeStruct((role_count * piece, tok_count), jnp.bfloat16)] * parts,
        name="pair_rows",
    )(places, *blocks)


def multiply(cot, features, tile):
    source_count, depth, tok_count = cot.shape
    width = sum(f.shape[2] for f in features)

    def kernel(cot_ref, *refs):
        left = jnp.concatenate([cot_ref[s] for s in range(source_count)], axis=1)
        at = 0
        for f_ref in refs[:-1]:
            f = f_ref[...].reshape(source_count * tok_count, f_ref.shape[2])
            refs[-1][:, at : at + f.shape[1]] = jnp.dot(left, f, preferred_element_type=jnp.float32)
            at += f.shape[1]

    return pl.pallas_call(
        kernel,
        grid=(depth // tile,),
        in_specs=[pl.BlockSpec((source_count, tile, tok_count), lambda i: (0, i, 0))]
        + [pl.BlockSpec(f.shape, lambda i: (0, 0, 0)) for f in features],
        out_specs=pl.BlockSpec((tile, width), lambda i: (i, 0)),
        out_shape=jax.ShapeDtypeStruct((depth, width), jnp.float32),
        compiler_params=pltpu.CompilerParams(vmem_limit_bytes=48 * 1024 * 1024),
        cost_estimate=pl.CostEstimate(
            flops=2 * depth * width * source_count * tok_count,
            bytes_accessed=depth * width * 4 + source_count * tok_count * (width + depth) * 2,
            transcendentals=0,
        ),
        name="multiply",
    )(cot, *features)


def finish(pieces, shift, odd, width):
    rows = pieces[0].shape[0]
    count = len(pieces)

    def kernel(odd_ref, *refs):
        for p in range(count):
            even_cols = refs[p][:, :width]
            odd_cols = refs[p][:, shift : shift + width]
            refs[-1][p * rows : (p + 1) * rows] = jnp.where(odd_ref[0] == 1, odd_cols, even_cols)

    return pl.pallas_call(
        kernel,
        in_specs=[pl.BlockSpec(memory_space=pltpu.SMEM)]
        + [pl.BlockSpec(memory_space=pltpu.VMEM)] * count,
        out_specs=pl.BlockSpec(memory_space=pltpu.VMEM),
        out_shape=jax.ShapeDtypeStruct((rows * count, width), jnp.float32),
        compiler_params=pltpu.CompilerParams(vmem_limit_bytes=32 * 1024 * 1024),
        name="finish",
    )(odd, *pieces)


def body(hidden_rows, lengths, balance, cotangent):
    role_count = lax.axis_size("role")
    dev_count = lax.axis_size("dev")
    role, dev = lax.axis_index("role"), lax.axis_index("dev")
    tok_count, width_in = hidden_rows.shape
    seq_count = lengths.shape[1]
    slot_len = tok_count // seq_count
    block_count = balance.shape[0]
    block_rows = tok_count // block_count
    pair_count = cotangent.shape[0] // role_count
    capacity = pair_count // block_rows
    slice_width = width_in // dev_count
    shift = slice_width % 128
    window = slice_width + shift
    starts = [slice_width * d - shift * (d % 2) for d in range(dev_count)]

    hops = jnp.arange(role_count, dtype=jnp.int32)
    blocks = sort_blocks(cotangent, (role + hops) % role_count, role_count)
    blocks = [blocks[0]] + [
        lax.ppermute(
            blocks[j], "role", [(r, (r + j) % role_count) for r in range(role_count)]
        )
        for j in range(1, role_count)
    ]

    groups = balance[:, 0]
    onehot = (groups[:, None] == hops[None, :]).astype(jnp.int32)
    earlier = jnp.cumsum(onehot, axis=0) - onehot
    block_rank = jnp.sum(earlier * onehot, axis=1)
    token = jnp.arange(tok_count, dtype=jnp.int32)
    row_of_token = jnp.repeat(block_rank, block_rows) * block_rows + token % block_rows
    group_of_token = jnp.repeat(groups, block_rows)
    keeping = token % slot_len < jnp.repeat(lengths[0], slot_len)
    rows = jnp.arange(pair_count, dtype=jnp.int32)
    from_group = (role - hops) % role_count
    places = (
        (from_group[:, None, None] == group_of_token[None, None, :])
        & (rows[None, :, None] == row_of_token[None, None, :])
        & keeping[None, None, :]
    ).astype(jnp.bfloat16)

    early = windows(hidden_rows, starts, FIRST_COLS)
    late = windows(hidden_rows, [s + FIRST_COLS for s in starts], window - FIRST_COLS)
    exchange = functools.partial(
        lax.all_to_all, axis_name="dev", split_axis=0, concat_axis=0, tiled=True
    )
    early = exchange(early)
    blocks = lax.optimization_barrier((blocks, early))[0]
    paired = pair_rows(blocks, places, role_count, PARTS)
    paired, late = lax.optimization_barrier((paired, late))
    gathered = [lax.all_gather(p, "dev", axis=0, tiled=False) for p in paired]
    late = exchange(late)

    pieces = []
    for cot in gathered:
        partial = multiply(cot, [early, late], cot.shape[1] // 4)
        pieces.append(lax.psum_scatter(partial, "role", scatter_dimension=0, tiled=True))
    return finish(pieces, shift, (dev % 2).reshape(1), slice_width)


def solution(mesh):
    in_specs = (
        P(("role", "dev"), None),
        P(("role", "dev"), None),
        P(("role", "dev"), None),
        P(("role", "dev"), None),
    )
    out_specs = P("role", "dev")
    return jax.shard_map(body, mesh=mesh, in_specs=in_specs, out_specs=out_specs, check_vma=False)
```

time: 413 us -> 475 us (1.15)
  waiting for transfers between devices: 104 us -> 294 us
  blocking collectives: 177 us -> 59.9 us
  Pallas kernels: 0 us -> 70.8 us
  local copies, waits for them, and re-layouts: 70.9 us -> 13 us
  matrix products: 40.1 us -> 0 us
  starting transfers between devices: 0.04 us -> 18.5 us
  other arithmetic: 6.41 us -> 1.56 us
    all_gather x1 -> x4, waiting for transfers between devices: 0.01 us -> 133 us  [body(): gathered = [lax.all_gather(p, 'dev', axis=0, tiled=False) for p in paired]]
    all_to_all x1, blocking collectives: 177 us -> 59.9 us  [body(): late = exchange(late)]
    pallas_call x0 -> x9, Pallas kernels: none -> 70.8 us  [the longest x4 39.2 us: multiply(): pl.pallas_call(kernel, grid=(depth // tile,), in_specs=[pl.BlockSpec((sou...]
    reduce_scatter x1 -> x4, waiting for transfers between devices: 103 us -> 152 us  [body(): lax.psum_scatter(partial, 'role', scatter_dimension=0, tiled=True)]
    dot_general x2 -> x0, matrix products: 40.1 us -> none  [the longest x1 32 us: body(): lax.dot_general(every_cot, features, (((0,), (0,)), ((), ())), preferred_...]
    reshape x4 -> x1, local copies, waits for them, and re-layouts: 35.2 us -> 0.09 us  [body(): keeping = token % slot_len < jnp.repeat(lengths[0], slot_len)]
    another operation x2 -> x0, local copies, waits for them, and re-layouts: 15.3 us -> none  [body(): outgoing.reshape(role_count, pair_rows, dev_count, slice_width)]
    ppermute x0 -> x7, starting transfers between devices: none -> 11.5 us  [body(): lax.ppermute(blocks[j], 'role', [(r, (r + j) % role_count) for r in range...]
  transfers between devices with their start and end apart: 2 -> 16, of which waited for: 1 -> 11; matrix products, arithmetic and copies ran while one was open for 16% -> 0% of each run, Pallas kernels for 0% -> 12%
where the time goes in v1:
time: 475 us; the launch traced here: 471 us
  waiting for transfers between devices  294 us (62%)
  Pallas kernels  70.8 us (15%)
  blocking collectives  59.9 us (13%)
  starting transfers between devices  18.5 us (4%)
  between operations  13.7 us (3%)
  local copies, waits for them, and re-layouts  13 us (3%)
    reduce_scatter x4, waiting for transfers between devices, body(): lax.psum_scatter(partial, 'role', scatter_dimension=0, tiled=True)  152 us
    all_gather x4, waiting for transfers between devices, body(): gathered = [lax.all_gather(p, 'dev', axis=0, tiled=False) for p in paired]  133 us
    all_to_all x1, blocking collectives, body(): late = exchange(late)  59.9 us
    pallas_call x4, Pallas kernels, multiply(): pl.pallas_call(kernel, grid=(depth // tile,), in_specs=[pl.BlockSpec((sou...  39.2 us
    pallas_call x2, Pallas kernels, windows(): pl.pallas_call(kernel, grid=(dev_count,), in_specs=[pl.BlockSpec((pl.Elem...  19.5 us
    unnamed x38, local copies, waits for them, and re-layouts  12.5 us
    ppermute x7, starting transfers between devices, body(): lax.ppermute(blocks[j], 'role', [(r, (r + j) % role_count) for r in range...  11.5 us
  transfers between devices with their start and end apart: 16, of which 11 were waited for; matrix products, arithmetic and copies ran while one was open for 0% of the time, Pallas kernels for 12%

profile of v1, /device:TPU:1, one launch (start us, length us, event | category | flops | bytes accessed | tf_op | source)
XLA Modules:
  0.0 471.3 jit_solution(13941223497132213328)
XLA Ops:
  6.5 0.5 and_select_fusion
  7.1 4.3 sort_blocks.1
  11.3 3.0 collective-permute-start
  14.3 1.6 collective-permute-start.1
  16.0 2.1 collective-permute-start.2
  18.0 2.3 collective-permute-start.4
  20.3 9.3 %cut_windows.2 = bf16[16,128,384]{2,1,0:T(8,128)(2,1)} custom-call(bf16[128,21504]{1,0:T(8,128)(2,1)} %rows_ref.3), custom_call_target="tpu_custom_call" | custom-call | tf_op jit(solution)/shard_map/cut_windows/pallas_call | solution.py:26
  29.6 6.7 %all-to-all-start = ((bf16[16,128,384]{2,1,0:T(8,128)(2,1)}), bf16[16,128,384]{2,1,0:T(8,128)(2,1)S(1)}, u32[]{:S(2)}, u32[]{:S(2)}) async-start(bf16[16,128,384]{2,1,0:T(8,128)(2,1)} %cut_windows.2), calls=%async_computation | async-start | bytes 3145728 | tf_op jit(solution)/shard_map/all_to_all | solution.py:194
  36.4 0.0 all-gather.15.cloned.1.call-start
  36.4 0.1 fusion
  36.5 10.2 %cut_windows.3 = bf16[16,128,1024]{2,1,0:T(8,128)(2,1)} custom-call(bf16[128,21504]{1,0:T(8,128)(2,1)} %rows_ref.3), custom_call_target="tpu_custom_call" | custom-call | tf_op jit(solution)/shard_map/cut_windows/pallas_call | solution.py:26
  46.7 0.1 reduce_window_sum.11
  46.8 0.2 select_reduce_fusion
  47.0 0.1 broadcast_in_dim.7
  47.0 0.1 mul.22
  47.1 0.1 broadcast_in_dim.6
  47.2 0.1 eq.60
  47.3 0.1 broadcast_in_dim.16
  47.4 0.1 reshape.110
  47.5 0.1 broadcast_compare_fusion
  47.6 0.9 collective-permute-start.5
  48.5 1.6 collective-permute-start.6
  50.1 0.6 and_convert_fusion.places_ref
  50.8 1.5 collective-permute-done.5.refs_6_
  52.2 3.7 collective-permute-done.6.refs_7_
  55.9 1.9 all-to-all-done.refs_0_
  57.8 4.9 %pair_rows.1 = (bf16[896,128]{1,0:T(8,128)(2,1)}, bf16[896,128]{1,0:T(8,128)(2,1)}, bf16[896,128]{1,0:T(8,128)(2,1)}, bf16[896,128]{1,0:T(8,128)(2,1)}) custom-call(bf16[8,20,128]{2,1,0:T(8,128)(2,1)} %and_convert_fusion.places_ref, bf16[20,3584]{1,0:T(8,128)(2,1)} %get-tuple-element.38.refs_0_, bf16[20,3584]{1,0:T(8,128)(2,1)} %copy-done.8, ...), custom_call_target="tpu_custom_call" | custom-call | tf_op jit(solution)/shard_map/pair_rows/pallas_call | solution.py:87
  62.8 0.0 all-gather.15.cloned.1.call-update
  62.8 0.0 all-gather.13.cloned.1.call-start
  62.9 0.7 all-gather.13.cloned.1.call-update
  63.6 0.0 all-gather.11.cloned.1.call-start
  63.6 0.7 all-gather.11.cloned.1.call-update
  64.3 0.0 all-gather.9.cloned.1.call-start
  64.3 0.5 all-gather.9.cloned.1.call-update
  64.9 0.0 reduce-scatter.11.cloned.1.call-start
  64.9 59.9 %all_to_all.10.refs_1_ = bf16[16,128,1024]{2,1,0:T(8,128)(2,1)} all-to-all(bf16[16,128,1024]{2,1,0:T(8,128)(2,1)} %cut_windows.3), channel_id=1, replica_groups=mesh['role'=8,'dev'=16] {'dev'}, dimensions={0} | all-to-all | bytes 8388608 | tf_op jit(solution)/shard_map/all_to_all | solution.py:199
  124.8 15.9 %all-gather.15.cloned.1.call-done = bf16[14336,128]{1,0:T(8,128)(2,1)} async-done(((bf16[896,128]{1,0:T(8,128)(2,1)}), bf16[14336,128]{1,0:T(8,128)(2,1)}) %all-gather.15.cloned.1.call-update) | async-done | bytes 3670032 | tf_op jit(solution)/shard_map/all_gather | solution.py:198
  140.7 2.0 copy-done.7
  142.7 9.8 %multiply.7 = f32[896,1408]{1,0:T(8,128)} custom-call(bf16[16,896,128]{2,1,0:T(8,128)(2,1)S(1)} %bitcast.10, bf16[16,128,384]{2,1,0:T(8,128)(2,1)S(1)} %all-to-all-done.refs_0_, bf16[16,128,1024]{2,1,0:T(8,128)(2,1)} %all_to_all.10.refs_1_), custom_call_target="tpu_custom_call" | custom-call | flops 5167382528 | bytes 14483456 | tf_op jit(solution)/shard_map/multiply/pallas_call | solution.py:110
  152.5 0.0 reduce-scatter.11.cloned.1.call-update
  152.6 0.0 reduce-scatter.9.cloned.1.call-start
  152.6 39.5 %all-gather.13.cloned.1.call-done = bf16[14336,128]{1,0:T(8,128)(2,1)} async-done(((bf16[896,128]{1,0:T(8,128)(2,1)}), bf16[14336,128]{1,0:T(8,128)(2,1)}) %all-gather.13.cloned.1.call-update) | async-done | bytes 3670032 | tf_op jit(solution)/shard_map/all_gather | solution.py:198
  192.1 2.0 copy-done.6
  194.1 9.8 %multiply.6 = f32[896,1408]{1,0:T(8,128)} custom-call(bf16[16,896,128]{2,1,0:T(8,128)(2,1)S(1)} %bitcast.9, bf16[16,128,384]{2,1,0:T(8,128)(2,1)S(1)} %all-to-all-done.refs_0_, bf16[16,128,1024]{2,1,0:T(8,128)(2,1)} %all_to_all.10.refs_1_), custom_call_target="tpu_custom_call" | custom-call | flops 5167382528 | bytes 14483456 | tf_op jit(solution)/shard_map/multiply/pallas_call | solution.py:110
  203.9 0.0 reduce-scatter.9.cloned.1.call-update
  203.9 0.0 reduce-scatter.7.cloned.1.call-start
  204.0 39.0 %all-gather.11.cloned.1.call-done = bf16[14336,128]{1,0:T(8,128)(2,1)} async-done(((bf16[896,128]{1,0:T(8,128)(2,1)}), bf16[14336,128]{1,0:T(8,128)(2,1)}) %all-gather.11.cloned.1.call-update) | async-done | bytes 3670032 | tf_op jit(solution)/shard_map/all_gather | solution.py:198
  243.0 2.0 copy-done.5
  245.1 9.8 %multiply.5 = f32[896,1408]{1,0:T(8,128)} custom-call(bf16[16,896,128]{2,1,0:T(8,128)(2,1)S(1)} %bitcast.8, bf16[16,128,384]{2,1,0:T(8,128)(2,1)S(1)} %all-to-all-done.refs_0_, bf16[16,128,1024]{2,1,0:T(8,128)(2,1)} %all_to_all.10.refs_1_), custom_call_target="tpu_custom_call" | custom-call | flops 5167382528 | bytes 14483456 | tf_op jit(solution)/shard_map/multiply/pallas_call | solution.py:110
  254.9 0.0 reduce-scatter.7.cloned.1.call-update
  254.9 0.0 reduce-scatter.5.cloned.1.call-start
  254.9 38.9 %all-gather.9.cloned.1.call-done = bf16[14336,128]{1,0:T(8,128)(2,1)} async-done(((bf16[896,128]{1,0:T(8,128)(2,1)}), bf16[14336,128]{1,0:T(8,128)(2,1)}) %all-gather.9.cloned.1.call-update) | async-done | bytes 3670032 | tf_op jit(solution)/shard_map/all_gather | solution.py:198
  293.8 2.0 copy-done.4
  295.8 9.8 %multiply.4 = f32[896,1408]{1,0:T(8,128)} custom-call(bf16[16,896,128]{2,1,0:T(8,128)(2,1)S(1)} %bitcast.7, bf16[16,128,384]{2,1,0:T(8,128)(2,1)S(1)} %all-to-all-done.refs_0_, bf16[16,128,1024]{2,1,0:T(8,128)(2,1)} %all_to_all.10.refs_1_), custom_call_target="tpu_custom_call" | custom-call | flops 5167382528 | bytes 14483456 | tf_op jit(solution)/shard_map/multiply/pallas_call | solution.py:110
  305.6 0.0 reduce-scatter.5.cloned.1.call-update
  305.7 27.1 %reduce-scatter.11.cloned.1.call-done.refs_3_ = f32[112,1408]{1,0:T(8,128)} async-done(((f32[896,1408]{1,0:T(8,128)}), f32[112,1408]{1,0:T(8,128)}) %reduce-scatter.11.cloned.1.call-update) | async-done | bytes 630800 | tf_op jit(solution)/shard_map/reduce_scatter | solution.py:204
  332.8 41.5 %reduce-scatter.9.cloned.1.call-done.refs_2_ = f32[112,1408]{1,0:T(8,128)} async-done(((f32[896,1408]{1,0:T(8,128)}), f32[112,1408]{1,0:T(8,128)}) %reduce-scatter.9.cloned.1.call-update) | async-done | bytes 630800 | tf_op jit(solution)/shard_map/reduce_scatter | solution.py:204
  374.3 41.4 %reduce-scatter.7.cloned.1.call-done.refs_1_ = f32[112,1408]{1,0:T(8,128)} async-done(((f32[896,1408]{1,0:T(8,128)}), f32[112,1408]{1,0:T(8,128)}) %reduce-scatter.7.cloned.1.call-update) | async-done | bytes 630800 | tf_op jit(solution)/shard_map/reduce_scatter | solution.py:204
  415.7 41.6 %reduce-scatter.5.cloned.1.call-done.refs_0_ = f32[112,1408]{1,0:T(8,128)} async-done(((f32[896,1408]{1,0:T(8,128)}), f32[112,1408]{1,0:T(8,128)}) %reduce-scatter.5.cloned.1.call-update) | async-done | bytes 630800 | tf_op jit(solution)/shard_map/reduce_scatter | solution.py:204
  457.3 1.1 copy-done
  458.3 1.1 copy-done.1
  459.4 1.1 copy-done.2
  460.5 1.1 copy-done.3
  461.6 2.8 finish.1
  (40 shorter events, 0.1 us)
Async XLA Ops:
  11.3 36.3 %collective-permute-start = (bf16[20,3584]{1,0:T(8,128)(2,1)}, bf16[20,3584]{1,0:T(8,128)(2,1)S(1)}, u32[]{:S(2)}, u32[]{:S(2)}) collective-permute-start(bf16[20,3584]{1,0:T(8,128)(2,1)} %get-tuple-element.31), channel_id=1, source_target_pairs={{0,16},{16,32},{32,48},{48,64},{64,80},{80,96},{96,112},{112,0},{1... | collective-permute-start | bytes 430088 | tf_op jit(solution)/shard_map/ppermute | solution.py:167
  14.3 34.2 %collective-permute-start.1 = (bf16[20,3584]{1,0:T(8,128)(2,1)}, bf16[20,3584]{1,0:T(8,128)(2,1)S(1)}, u32[]{:S(2)}, u32[]{:S(2)}) collective-permute-start(bf16[20,3584]{1,0:T(8,128)(2,1)} %get-tuple-element.32), channel_id=1, source_target_pairs={{0,32},{16,48},{32,64},{48,80},{64,96},{80,112},{96,0},{112,16},{1... | collective-permute-start | bytes 430088 | tf_op jit(solution)/shard_map/ppermute | solution.py:167
  16.0 34.8 %collective-permute-start.2 = (bf16[20,3584]{1,0:T(8,128)(2,1)}, bf16[20,3584]{1,0:T(8,128)(2,1)S(1)}, u32[]{:S(2)}, u32[]{:S(2)}) collective-permute-start(bf16[20,3584]{1,0:T(8,128)(2,1)} %get-tuple-element.33), channel_id=1, source_target_pairs={{0,48},{16,64},{32,80},{48,96},{64,112},{80,0},{96,16},{112,32},{1... | collective-permute-start | bytes 430088 | tf_op jit(solution)/shard_map/ppermute | solution.py:167
  18.0 32.7 %collective-permute-start.3 = (bf16[20,3584]{1,0:T(8,128)(2,1)}, bf16[20,3584]{1,0:T(8,128)(2,1)S(1)}, u32[]{:S(2)}, u32[]{:S(2)}) collective-permute-start(bf16[20,3584]{1,0:T(8,128)(2,1)} %get-tuple-element.34), channel_id=1, source_target_pairs={{0,64},{16,80},{32,96},{48,112},{64,0},{80,16},{96,32},{112,48},{1... | collective-permute-start | bytes 430088 | tf_op jit(solution)/shard_map/ppermute | solution.py:167
  18.0 18.4 %copy-start.15 = (s32[32,1]{0,1:T(1,128)S(1)}, s32[32,1]{0,1:T(1,128)}, u32[]{:S(2)}) copy-start(s32[32,1]{0,1:T(1,128)} %param.6) | copy-start | bytes 388
  18.0 32.7 %collective-permute-start.4 = (bf16[20,3584]{1,0:T(8,128)(2,1)}, bf16[20,3584]{1,0:T(8,128)(2,1)S(1)}, u32[]{:S(2)}, u32[]{:S(2)}) collective-permute-start(bf16[20,3584]{1,0:T(8,128)(2,1)} %get-tuple-element.35), channel_id=1, source_target_pairs={{0,80},{16,96},{32,112},{48,0},{64,16},{80,32},{96,48},{112,64},{1... | collective-permute-start | bytes 430088 | tf_op jit(solution)/shard_map/ppermute | solution.py:167
  29.6 28.2 %all-to-all-start = ((bf16[16,128,384]{2,1,0:T(8,128)(2,1)}), bf16[16,128,384]{2,1,0:T(8,128)(2,1)S(1)}, u32[]{:S(2)}, u32[]{:S(2)}) async-start(bf16[16,128,384]{2,1,0:T(8,128)(2,1)} %cut_windows.2), calls=%async_computation | async-start | bytes 3145728 | tf_op jit(solution)/shard_map/all_to_all | solution.py:194
  36.4 104.3 %all-gather.15.cloned.1.call-start = ((), (), s32[]{:S(2)}) async-start(), calls=%async_computation.13 | async-start | bytes 3899392 | tf_op jit(solution)/shard_map/all_gather | solution.py:198
  36.5 10.8 %copy-start.16 = (s32[1,4]{1,0:T(1,128)S(1)}, s32[1,4]{1,0:T(1,128)}, u32[]{:S(2)}) copy-start(s32[1,4]{1,0:T(1,128)} %param.5) | copy-start | bytes 52
  36.5 11.1 %copy-start.18 = (bf16[20,3584]{1,0:T(8,128)(2,1)S(1)}, bf16[20,3584]{1,0:T(8,128)(2,1)}, u32[]{:S(2)}) copy-start(bf16[20,3584]{1,0:T(8,128)(2,1)} %get-tuple-element.36) | copy-start | bytes 430084
  36.5 12.0 %copy-start.17 = (bf16[20,3584]{1,0:T(8,128)(2,1)S(1)}, bf16[20,3584]{1,0:T(8,128)(2,1)}, u32[]{:S(2)}) copy-start(bf16[20,3584]{1,0:T(8,128)(2,1)} %get-tuple-element.37) | copy-start | bytes 430084
  47.6 10.2 %copy-start.8 = (bf16[20,3584]{1,0:T(8,128)(2,1)}, bf16[20,3584]{1,0:T(8,128)(2,1)S(1)}, u32[]{:S(2)}) copy-start(bf16[20,3584]{1,0:T(8,128)(2,1)S(1)} %collective-permute-done.refs_1_) | copy-start | bytes 430084
  47.6 4.6 collective-permute-start.5
  48.5 9.3 %copy-start.9 = (bf16[20,3584]{1,0:T(8,128)(2,1)}, bf16[20,3584]{1,0:T(8,128)(2,1)S(1)}, u32[]{:S(2)}) copy-start(bf16[20,3584]{1,0:T(8,128)(2,1)S(1)} %collective-permute-done.1.refs_2_) | copy-start | bytes 430084
  48.5 7.4 %collective-permute-start.6 = (bf16[20,3584]{1,0:T(8,128)(2,1)S(1)}, bf16[20,3584]{1,0:T(8,128)(2,1)S(1)}, u32[]{:S(2)}, u32[]{:S(2)}) collective-permute-start(bf16[20,3584]{1,0:T(8,128)(2,1)S(1)} %copy-done.17), channel_id=1, source_target_pairs={{0,112},{16,0},{32,16},{48,32},{64,48},{80,64},{96,80},{112,96},{1... | collective-permute-start | bytes 430088 | tf_op jit(solution)/shard_map/ppermute | solution.py:167
  50.7 7.1 %copy-start.10 = (bf16[20,3584]{1,0:T(8,128)(2,1)}, bf16[20,3584]{1,0:T(8,128)(2,1)S(1)}, u32[]{:S(2)}) copy-start(bf16[20,3584]{1,0:T(8,128)(2,1)S(1)} %collective-permute-done.2.refs_3_) | copy-start | bytes 430084
  50.7 7.0 %copy-start.11 = (bf16[20,3584]{1,0:T(8,128)(2,1)}, bf16[20,3584]{1,0:T(8,128)(2,1)S(1)}, u32[]{:S(2)}) copy-start(bf16[20,3584]{1,0:T(8,128)(2,1)S(1)} %collective-permute-done.3.refs_4_) | copy-start | bytes 430084
  50.8 7.0 %copy-start.12 = (bf16[20,3584]{1,0:T(8,128)(2,1)}, bf16[20,3584]{1,0:T(8,128)(2,1)S(1)}, u32[]{:S(2)}) copy-start(bf16[20,3584]{1,0:T(8,128)(2,1)S(1)} %collective-permute-done.4.refs_5_) | copy-start | bytes 430084
  52.2 5.6 %copy-start.13 = (bf16[20,3584]{1,0:T(8,128)(2,1)}, bf16[20,3584]{1,0:T(8,128)(2,1)S(1)}, u32[]{:S(2)}) copy-start(bf16[20,3584]{1,0:T(8,128)(2,1)S(1)} %collective-permute-done.5.refs_6_) | copy-start | bytes 430084
  55.9 1.9 copy-start.14
  62.8 129.3 %all-gather.13.cloned.1.call-start = ((), (), s32[]{:S(2)}) async-start(), calls=%async_computation.12 | async-start | bytes 3899392 | tf_op jit(solution)/shard_map/all_gather | solution.py:198
  63.6 179.5 %all-gather.11.cloned.1.call-start = ((), (), s32[]{:S(2)}) async-start(), calls=%async_computation.11 | async-start | bytes 3899392 | tf_op jit(solution)/shard_map/all_gather | solution.py:198
  64.3 229.5 %all-gather.9.cloned.1.call-start = ((), (), s32[]{:S(2)}) async-start(), calls=%async_computation.10 | async-start | bytes 3899392 | tf_op jit(solution)/shard_map/all_gather | solution.py:198
  64.9 267.9 %reduce-scatter.11.cloned.1.call-start = ((), (), s32[]{:S(2)}) async-start(), calls=%async_computation.9 | async-start | bytes 5677056 | tf_op jit(solution)/shard_map/reduce_scatter | solution.py:204
  140.7 2.0 copy-start.7
  152.6 221.8 %reduce-scatter.9.cloned.1.call-start = ((), (), s32[]{:S(2)}) async-start(), calls=%async_computation.8 | async-start | bytes 5677056 | tf_op jit(solution)/shard_map/reduce_scatter | solution.py:204
  192.1 2.0 copy-start.6
  203.9 211.7 %reduce-scatter.7.cloned.1.call-start = ((), (), s32[]{:S(2)}) async-start(), calls=%async_computation.7 | async-start | bytes 5677056 | tf_op jit(solution)/shard_map/reduce_scatter | solution.py:204
  243.0 2.0 copy-start.5
  254.9 202.4 %reduce-scatter.5.cloned.1.call-start = ((), (), s32[]{:S(2)}) async-start(), calls=%async_computation.6 | async-start | bytes 5677056 | tf_op jit(solution)/shard_map/reduce_scatter | solution.py:204
  293.8 2.0 copy-start.4
  457.3 1.1 copy-start
  458.3 1.1 copy-start.1
  459.4 1.1 copy-start.2
  460.5 1.1 copy-start.3
Sparse Core Ops, SparseCore 0:
  62.9 77.7 all-gather.14
  142.8 49.2 all-gather.12
  194.2 48.7 all-gather.10
  245.0 48.7 all-gather.8
  296.1 36.6 reduce-scatter.10
  335.2 39.0 reduce-scatter.8
  376.8 38.8 reduce-scatter.6
  418.2 38.9 reduce-scatter.4

commit v2 on v0

v2 whole, which is shorter than its diff:
```python
import jax
import jax.numpy as jnp
from jax import lax
from jax.experimental import pallas as pl
from jax.experimental.pallas import tpu as pltpu
from jax.sharding import PartitionSpec as P

PARTS = (224, 224)
STEP = 112
SPANS = (512, 896)
FINE = 256.0
TOP = 32767.0
SIDE = 4
VMEM = pl.BlockSpec(memory_space=pltpu.VMEM)
SMEM = pl.BlockSpec(memory_space=pltpu.SMEM)
ANY = pl.BlockSpec(memory_space=pl.ANY)
TINY = pl.CostEstimate(flops=1, bytes_accessed=1, transcendentals=0)


def params(mib):
    return pltpu.CompilerParams(vmem_limit_bytes=mib * 1024 * 1024)


def along_z(step, flip=0):
    return [
        (z * 2 + c, (z + step) % SIDE * 2 + (c + flip) % 2) for z in range(SIDE) for c in range(2)
    ]


def cut_windows(hidden_rows, starts, width):
    tok_count, width_in = hidden_rows.shape
    tile = 32

    def kernel(rows_ref, out_ref):
        for d, start in enumerate(starts):
            out_ref[d] = rows_ref[:, start : start + width]

    return pl.pallas_call(
        kernel,
        grid=(tok_count // tile,),
        in_specs=[pl.BlockSpec((tile, width_in), lambda i: (i, 0))],
        out_specs=pl.BlockSpec((len(starts), tile, width), lambda i: (0, i, 0)),
        out_shape=jax.ShapeDtypeStruct((len(starts), tok_count, width), hidden_rows.dtype),
        compiler_params=params(60),
        name="cut_windows",
    )(hidden_rows)


def hold(value, awaited):
    def kernel(value_ref, awaited_ref, out_ref):
        pass

    return pl.pallas_call(
        kernel,
        in_specs=[ANY, ANY],
        out_specs=ANY,
        out_shape=jax.ShapeDtypeStruct(value.shape, value.dtype),
        input_output_aliases={0: 0},
        compiler_params=params(60),
        cost_estimate=TINY,
        name="hold",
    )(value, awaited)


def sort_blocks(cotangent, targets):
    rows, width = cotangent.shape
    count = targets.shape[0]
    block = rows // count

    def kernel(targets_ref, cot_ref, *out_refs):
        row = lax.broadcasted_iota(jnp.int32, (block, rows), 0)
        column = lax.broadcasted_iota(jnp.int32, (block, rows), 1)
        for j in range(count):
            taking = (column == row + targets_ref[j] * block).astype(jnp.bfloat16)
            out_refs[j][...] = jnp.dot(
                taking, cot_ref[...], preferred_element_type=jnp.float32
            ).astype(jnp.bfloat16)

    return pl.pallas_call(
        kernel,
        in_specs=[SMEM, VMEM],
        out_specs=[VMEM] * count,
        out_shape=[jax.ShapeDtypeStruct((block, width), cotangent.dtype)] * count,
        compiler_params=params(60),
        name="sort_blocks",
    )(targets, cotangent)


def pair_rows(core, blocks, places, *awaited):
    block, width = blocks[0].shape
    count = len(blocks)
    tok_count = places.shape[2]
    share = width // count

    def kernel(core_ref, places_ref, *refs):
        ins, outs = refs[:count], refs[-len(PARTS) :]
        z = pl.program_id(0)
        total = jnp.zeros((2 * share, tok_count), jnp.float32)
        for j in range(count):
            total += lax.dot_general(
                ins[j][...],
                places_ref[j],
                (((0,), (0,)), ((), ())),
                preferred_element_type=jnp.float32,
            )
        total = total.astype(jnp.bfloat16)
        for q in range(2):
            own = jnp.where(core_ref[0] == q, 1, 0)
            at = q * share
            for m, out in zip(PARTS, outs, strict=True):
                to = pl.multiple_of((own * SIDE + z) * m, 16)
                out[pl.ds(to, m)] = total[at : at + m]
                at += m

    return pl.pallas_call(
        kernel,
        grid=(SIDE,),
        in_specs=[SMEM, pl.BlockSpec((count, block, tok_count), lambda i: (0, 0, 0))]
        + [pl.BlockSpec((block, 2 * share), lambda i: (0, i))] * count
        + [ANY] * len(awaited),
        out_specs=[pl.BlockSpec((count * m, tok_count), lambda i: (0, 0)) for m in PARTS],
        out_shape=[jax.ShapeDtypeStruct((count * m, tok_count), jnp.bfloat16) for m in PARTS],
        compiler_params=params(60),
        name="pair_rows",
    )(core, places, *blocks, *awaited)


def multiply(cot, features, *awaited):
    source_count, rows, tok_count = cot.shape
    width = sum(f.shape[2] for f in features)
    steps = 4
    tile = rows // steps

    def kernel(cot_ref, *refs):
        left = jnp.concatenate([cot_ref[i] for i in range(source_count)], axis=1)

        def dots(out):
            at = 0
            for f_ref in refs[: len(features)]:
                span = f_ref.shape[2]
                right = f_ref[...].reshape(source_count * tok_count, span)
                out[:, at : at + span] = jnp.dot(left, right, preferred_element_type=jnp.float32)
                at += span

        for core, out in enumerate(refs[-2:]):

            @pl.when(pl.program_id(0) // (steps // 2) == core)
            def _(out=out):
                dots(out)

    return pl.pallas_call(
        kernel,
        grid=(steps,),
        in_specs=[pl.BlockSpec((source_count, tile, tok_count), lambda i: (0, i, 0))]
        + [pl.BlockSpec(f.shape, lambda i: (0, 0, 0)) for f in features]
        + [ANY] * len(awaited),
        out_specs=[
            pl.BlockSpec((tile, width), lambda i: (jnp.minimum(i, steps // 2 - 1), 0)),
            pl.BlockSpec((tile, width), lambda i: (jnp.maximum(i - steps // 2, 0), 0)),
        ],
        out_shape=[jax.ShapeDtypeStruct((steps // 2 * tile, width), jnp.float32)] * 2,
        compiler_params=params(60),
        cost_estimate=TINY,
        name="multiply",
    )(cot, *features, *awaited)


def code(own, got, *awaited):
    rows, width = own.shape
    m = rows // SIDE

    def kernel(own_ref, got_ref, *refs):
        out = refs[-1]
        total = own_ref[...] + got_ref[...]
        largest = jnp.max(jnp.abs(total), axis=0, keepdims=True)
        level = jnp.ceil(jnp.log2(jnp.maximum(largest, 2.0**-125)) * FINE) + 1.0
        scaled = (total * jnp.exp2(level * (-1.0 / FINE))) * TOP
        coded = jnp.round(jnp.clip(scaled, -TOP, TOP)).astype(jnp.int32)
        out[0, :m] = coded.astype(jnp.int16)
        out[0, m:] = jnp.broadcast_to(level.astype(jnp.int32), (16, width)).astype(jnp.int16)

    return pl.pallas_call(
        kernel,
        grid=(SIDE,),
        in_specs=[pl.BlockSpec((m, width), lambda i: (i, 0))] * 2 + [ANY] * len(awaited),
        out_specs=pl.BlockSpec((1, m + 16, width), lambda i: (i, 0, 0)),
        out_shape=jax.ShapeDtypeStruct((SIDE, m + 16, width), jnp.int16),
        compiler_params=params(60),
        cost_estimate=TINY,
        name="code",
    )(own, got, *awaited)


def finish(parts, odd, shift, width):
    counts = [m // STEP for m in PARTS]
    firsts = [sum(counts[:p]) for p in range(len(counts))]

    def kernel(odd_ref, *refs):
        out = refs[-1]
        for p, (first, count) in enumerate(zip(firsts, counts, strict=True)):
            rows, levels = refs[2 * p], refs[2 * p + 1]

            @pl.when((pl.program_id(0) >= first) & (pl.program_id(0) < first + count))
            def _(rows=rows, levels=levels):
                total = 0.0
                for z in range(SIDE):
                    level = levels[z].astype(jnp.int32).astype(jnp.float32)[:1]
                    scale = jnp.exp2(level * (1.0 / FINE)) * (1.0 / TOP)
                    total = total + rows[z].astype(jnp.int32).astype(jnp.float32) * scale
                out[...] = jnp.where(odd_ref[0] == 1, total[:, shift : shift + width], total[:, :width])

    specs, ins = [], []
    for part, m, first, count in zip(parts, PARTS, firsts, counts, strict=True):
        window = part.shape[2]

        def where(i, first=first, count=count):
            return 0, jnp.clip(i - first, 0, count - 1), 0

        def below(i, m=m):
            return 0, m // 16, 0

        specs += [pl.BlockSpec((SIDE, STEP, window), where), pl.BlockSpec((SIDE, 16, window), below)]
        ins += [part, part]
    return pl.pallas_call(
        kernel,
        grid=(sum(counts),),
        in_specs=[SMEM] + specs,
        out_specs=pl.BlockSpec((STEP, width), lambda i: (i, 0)),
        out_shape=jax.ShapeDtypeStruct((sum(PARTS), width), jnp.float32),
        compiler_params=params(60),
        name="finish",
    )(odd, *ins)


def body(hidden_rows, lengths, balance, cotangent):
    role_count = lax.axis_size("role")
    dev_count = lax.axis_size("dev")
    role, dev = lax.axis_index("role"), lax.axis_index("dev")
    z, core, y, x = role // 2, role % 2, dev // SIDE, dev % SIDE
    tok_count, width_in = hidden_rows.shape
    seq_count = lengths.shape[1]
    slot_len = tok_count // seq_count
    block_count = balance.shape[0]
    block_rows = tok_count // block_count
    pair_count = cotangent.shape[0] // role_count
    slice_width = width_in // dev_count
    shift = slice_width % 128
    starts = [slice_width * d - shift * (d % 2) for d in range(dev_count)]

    steps = [(dz, flip) for dz in range(SIDE) for flip in range(2)]
    ahead = jnp.stack([(z + dz) % SIDE * 2 + (core + flip) % 2 for dz, flip in steps])
    behind = jnp.stack([(z - dz) % SIDE * 2 + (core + flip) % 2 for dz, flip in steps])
    blocks = sort_blocks(cotangent, ahead)
    blocks = [blocks[0]] + [
        lax.ppermute(block, "role", along_z(*step))
        for block, step in zip(blocks[1:], steps[1:], strict=True)
    ]

    groups = balance[:, 0]
    onehot = (groups[:, None] == jnp.arange(role_count, dtype=jnp.int32)[None, :]).astype(jnp.int32)
    earlier = jnp.cumsum(onehot, axis=0) - onehot
    block_rank = jnp.sum(earlier * onehot, axis=1)
    token = jnp.arange(tok_count, dtype=jnp.int32)
    row_of_token = jnp.repeat(block_rank, block_rows) * block_rows + token % block_rows
    group_of_token = jnp.repeat(groups, block_rows)
    keeping = token % slot_len < jnp.repeat(lengths[0], slot_len)
    rows = jnp.arange(pair_count, dtype=jnp.int32)
    places = (
        (behind[:, None, None] == group_of_token[None, None, :])
        & (rows[None, :, None] == row_of_token[None, None, :])
        & keeping[None, None, :]
    ).astype(jnp.bfloat16)

    def exchange(cut):
        return lax.all_to_all(cut, "dev", split_axis=0, concat_axis=0, tiled=True)

    early = exchange(cut_windows(hidden_rows, starts, SPANS[0]))
    late = cut_windows(hidden_rows, [start + SPANS[0] for start in starts], SPANS[1])
    paired = pair_rows(core.reshape(1), blocks, places, early, late)
    gathered = [lax.all_gather(cot, "dev", axis=0, tiled=False) for cot in paired]
    features = [early, exchange(hold(late, paired[0]))]

    planes = [[2 * i + c for i in range(SIDE)] for c in range(2)]
    coded, came = [], []
    for cot in gathered:
        other, own = multiply(cot, features, *came[-1:])
        got = lax.ppermute(other, "role", along_z(0, 1))
        coded.append(code(own, got, *came[-2:-1]))
        came.append(
            lax.all_to_all(
                coded[-1], "role", split_axis=0, concat_axis=0, axis_index_groups=planes, tiled=True
            )
        )
    return finish(came, (dev % 2).reshape(1), shift, slice_width)


def solution(mesh):
    in_specs = (
        P(("role", "dev"), None),
        P(("role", "dev"), None),
        P(("role", "dev"), None),
        P(("role", "dev"), None),
    )
    out_specs = P("role", "dev")
    return jax.shard_map(body, mesh=mesh, in_specs=in_specs, out_specs=out_specs, check_vma=False)
```

time: 413 us -> 308 us (0.75)
  blocking collectives: 177 us -> 56.1 us
  Pallas kernels: 0 us -> 72.5 us
  local copies, waits for them, and re-layouts: 70.9 us -> 5.61 us
  matrix products: 40.1 us -> 0 us
  starting transfers between devices: 0.04 us -> 27.7 us
  waiting for transfers between devices: 104 us -> 131 us
  other arithmetic: 6.41 us -> 1.04 us
    all_to_all x1, blocking collectives: 177 us -> 56.1 us  [exchange(): return lax.all_to_all(cut, 'dev', split_axis=0, concat_axis=0, tiled=True)]
    reduce_scatter x1 -> x0, waiting for transfers between devices: 103 us -> none  [body(): lax.psum_scatter(lax.dot_general(every_cot, features, (((0,), (0,)), ((),...]
    pallas_call x0 -> x10, Pallas kernels: none -> 72.5 us  [the longest x2 36.2 us: multiply(): pl.pallas_call(kernel, grid=(steps,), in_specs=[pl.BlockSpec((source_coun...]
    all_gather x1 -> x2, waiting for transfers between devices: 0.01 us -> 69.2 us  [body(): lax.all_gather(cot, 'dev', axis=0, tiled=False)]
    dot_general x2 -> x0, matrix products: 40.1 us -> none  [the longest x1 32 us: body(): lax.dot_general(every_cot, features, (((0,), (0,)), ((), ())), preferred_...]
    all_to_all x0 -> x3, waiting for transfers between devices: none -> 36.8 us  [the longest x2 34.4 us: body(): lax.all_to_all(coded[-1], 'role', split_axis=0, concat_axis=0, axis_index...]
    reshape x4 -> x1, local copies, waits for them, and re-layouts: 35.2 us -> 0.09 us  [body(): keeping = token % slot_len < jnp.repeat(lengths[0], slot_len)]
    ppermute x0 -> x9, waiting for transfers between devices: none -> 24 us  [the longest x2 16.7 us: body(): got = lax.ppermute(other, 'role', along_z(0, 1))]
  transfers between devices with their start and end apart: 2 -> 14, of which waited for: 1 -> 10; matrix products, arithmetic and copies ran while one was open for 16% -> 1% of each run, Pallas kernels for 0% -> 11%
where the time goes in v2:
time: 308 us; the launch traced here: 307 us
  waiting for transfers between devices  131 us (43%)
  Pallas kernels  72.5 us (24%)
  blocking collectives  56.1 us (18%)
  starting transfers between devices  27.7 us (9%)
  between operations  13.7 us (4%)
  local copies, waits for them, and re-layouts  5.61 us (2%)
    all_gather x2, waiting for transfers between devices, body(): lax.all_gather(cot, 'dev', axis=0, tiled=False)  69.2 us
    all_to_all x1, blocking collectives, exchange(): return lax.all_to_all(cut, 'dev', split_axis=0, concat_axis=0, tiled=True)  56.1 us
    pallas_call x2, Pallas kernels, multiply(): pl.pallas_call(kernel, grid=(steps,), in_specs=[pl.BlockSpec((source_coun...  36.2 us
    all_to_all x2, waiting for transfers between devices, body(): lax.all_to_all(coded[-1], 'role', split_axis=0, concat_axis=0, axis_index...  34.4 us
    ppermute x2, waiting for transfers between devices, body(): got = lax.ppermute(other, 'role', along_z(0, 1))  16.7 us
    pallas_call x2, Pallas kernels, code(): pl.pallas_call(kernel, grid=(SIDE,), in_specs=[pl.BlockSpec((m, width), l...  12.5 us
    ppermute x7, starting transfers between devices, body(): lax.ppermute(block, 'role', along_z(*step))  10 us
    pallas_call x2, Pallas kernels, cut_windows(): pl.pallas_call(kernel, grid=(tok_count // tile,), in_specs=[pl.BlockSpec(...  9.44 us
  transfers between devices with their start and end apart: 14, of which 10 were waited for; matrix products, arithmetic and copies ran while one was open for 1% of the time, Pallas kernels for 11%

profile of v2, /device:TPU:1, one launch (start us, length us, event | category | flops | bytes accessed | tf_op | source)
XLA Modules:
  0.0 307.3 jit_solution(12328458970394941208)
XLA Ops:
  6.5 4.4 %cut_windows.2 = bf16[16,128,512]{2,1,0:T(8,128)(2,1)} custom-call(bf16[128,21504]{1,0:T(8,128)(2,1)} %rows_ref.3), custom_call_target="tpu_custom_call" | custom-call | tf_op jit(solution)/shard_map/cut_windows/pallas_call | solution.py:38
  11.0 7.6 %all-to-all-start = ((bf16[16,128,512]{2,1,0:T(8,128)(2,1)}), bf16[16,128,512]{2,1,0:T(8,128)(2,1)S(1)}, u32[]{:S(2)}, u32[]{:S(2)}) async-start(bf16[16,128,512]{2,1,0:T(8,128)(2,1)} %cut_windows.2), calls=%async_computation | async-start | bytes 4194304 | tf_op jit(solution)/shard_map/all_to_all | solution.py:275
  18.6 0.0 all-gather.5.cloned.1.call-start
  18.7 0.7 stack.65.targets_ref
  19.4 3.3 %sort_blocks.1 = (bf16[20,3584]{1,0:T(8,128)(2,1)}, bf16[20,3584]{1,0:T(8,128)(2,1)}, bf16[20,3584]{1,0:T(8,128)(2,1)}, bf16[20,3584]{1,0:T(8,128)(2,1)}, bf16[2...) custom-call(s32[8]{0:T(128)} %stack.65.targets_ref, ...), custom_call_target="tpu_custom_call" | custom-call | tf_op jit(solution)/shard_map/sort_blocks/pallas_call | solution.py:79
  22.7 1.1 collective-permute-start
  23.8 1.5 collective-permute-start.1
  25.3 1.8 collective-permute-start.2
  27.1 1.7 collective-permute-start.3
  28.8 1.7 collective-permute-start.4
  30.4 5.0 %cut_windows.3.refs_9_.value_ref = bf16[16,128,896]{2,1,0:T(8,128)(2,1)} custom-call(bf16[128,21504]{1,0:T(8,128)(2,1)} %rows_ref.3), custom_call_target="tpu_custom_call" | custom-call | tf_op jit(solution)/shard_map/cut_windows/pallas_call | solution.py:38
  35.5 0.0 copy-done.10
  35.5 0.1 broadcast_in_dim.6
  35.5 0.1 eq.90
  35.6 0.1 fusion
  35.7 0.1 reduce_window_sum.11
  35.8 0.2 select_reduce_fusion
  36.0 0.1 broadcast_in_dim.7
  36.0 0.1 mul.56
  36.1 0.0 copy-done.11
  36.2 0.1 broadcast_in_dim.16
  36.2 0.1 reshape.98
  36.3 0.1 stack.58
  36.4 0.1 broadcast_compare_fusion
  36.5 0.0 collective-permute-done.refs_1_
  36.5 0.0 copy-start.3
  36.5 1.1 collective-permute-start.5
  37.6 0.0 collective-permute-done.1.refs_2_
  37.6 0.0 copy-done.12
  37.6 1.2 collective-permute-start.6
  38.8 0.6 and_convert_fusion.places_ref
  39.4 0.0 collective-permute-done.2.refs_3_
  39.5 1.5 collective-permute-done.3.refs_4_
  40.9 3.8 %collective-permute-done.4.refs_5_ = bf16[20,3584]{1,0:T(8,128)(2,1)S(1)} collective-permute-done((bf16[20,3584]{1,0:T(8,128)(2,1)}, bf16[20,3584]{1,0:T(8,128)(2,1)S(1)}, u32[]{:S(2)}, u32[]{:S(2)}) %collective-permute-start.4) | collective-permute-done | bytes 143392 | tf_op jit(solution)/shard_map/ppermute | solution.py:255
  44.7 0.0 collective-permute-done.5.refs_6_
  44.7 2.0 collective-permute-done.6.refs_7_
  46.7 2.3 all-to-all-done.refs_8_.refs_0_
  49.0 0.0 copy-done.3
  49.0 0.0 copy-done.4
  49.0 0.0 copy-done.5
  49.1 0.0 copy-done.6
  49.1 1.3 copy-done.1
  50.4 5.1 %pair_rows.1 = (bf16[1792,128]{1,0:T(8,128)(2,1)}, bf16[1792,128]{1,0:T(8,128)(2,1)}) custom-call(s32[1]{0:T(128)} %bitcast.1.core_ref, bf16[8,20,128]{2,1,0:T(8,128)(2,1)} %and_convert_fusion.places_ref, bf16[20,3584]{1,0:T(8,128)(2,1)} %get-tuple-element.19.refs_0_, bf16[20,3584]{1,0:T(8,128)(2,1)} %copy-done.3, bf16[20,3584]{1,0:T(8,128)(2,1)} %copy-done.4, ...), custom_call_target="tpu_custom_call" | custom-call | tf_op jit(solution)/shard_map/pair_rows/pallas_call | solution.py:115
  55.5 0.0 all-gather.5.cloned.1.call-update
  55.5 0.0 all-gather.7.cloned.1.call-start
  55.5 0.7 all-gather.7.cloned.1.call-update
  56.3 56.1 %all_to_all.20.refs_1_ = bf16[16,128,896]{2,1,0:T(8,128)(2,1)} all-to-all(bf16[16,128,896]{2,1,0:T(8,128)(2,1)} %hold.1), channel_id=1, replica_groups=mesh['role'=8,'dev'=16] {'dev'}, dimensions={0} | all-to-all | bytes 7340032 | tf_op jit(solution)/shard_map/all_to_all | solution.py:275
  112.4 38.9 %all-gather.5.cloned.1.call-done = bf16[28672,128]{1,0:T(8,128)(2,1)} async-done(((bf16[1792,128]{1,0:T(8,128)(2,1)}), bf16[28672,128]{1,0:T(8,128)(2,1)}) %all-gather.5.cloned.1.call-update) | async-done | bytes 7340048 | tf_op jit(solution)/shard_map/all_gather | solution.py:280
  151.3 18.1 %multiply.2 = (f32[896,1408]{1,0:T(8,128)}, f32[896,1408]{1,0:T(8,128)}) custom-call(bf16[16,1792,128]{2,1,0:T(8,128)(2,1)} %bitcast.21, bf16[16,128,512]{2,1,0:T(8,128)(2,1)} %copy-done.1, bf16[16,128,896]{2,1,0:T(8,128)(2,1)} %all_to_all.20.refs_1_), custom_call_target="tpu_custom_call" | custom-call | flops 1 | bytes 1 | tf_op jit(solution)/shard_map/multiply/pallas_call | solution.py:151
  169.4 0.7 collective-permute-start.7
  170.1 8.3 %collective-permute-done.7.got_ref = f32[896,1408]{1,0:T(8,128)} collective-permute-done((f32[896,1408]{1,0:T(8,128)}, f32[896,1408]{1,0:T(8,128)}, u32[]{:S(2)}, u32[]{:S(2)}) %collective-permute-start.7) | collective-permute-done | bytes 5046304 | tf_op jit(solution)/shard_map/ppermute | solution.py:287
  178.4 6.3 %code.2 = s16[4,240,1408]{2,1,0:T(8,128)(2,1)} custom-call(f32[896,1408]{1,0:T(8,128)} %get-tuple-element.28.own_ref, f32[896,1408]{1,0:T(8,128)} %collective-permute-done.7.got_ref), custom_call_target="tpu_custom_call" | custom-call | flops 1 | bytes 1 | tf_op jit(solution)/shard_map/code/pallas_call | solution.py:182
  184.7 4.1 %all-to-all-start.2 = ((s16[4,240,1408]{2,1,0:T(8,128)(2,1)}), s16[4,240,1408]{2,1,0:T(8,128)(2,1)S(1)}, u32[]{:S(2)}, u32[]{:S(2)}) async-start(s16[4,240,1408]{2,1,0:T(8,128)(2,1)} %code.2), calls=%async_computation.2 | async-start | bytes 5406720 | tf_op jit(solution)/shard_map/all_to_all | solution.py:290
  188.8 30.3 %all-gather.7.cloned.1.call-done = bf16[28672,128]{1,0:T(8,128)(2,1)} async-done(((bf16[1792,128]{1,0:T(8,128)(2,1)}), bf16[28672,128]{1,0:T(8,128)(2,1)}) %all-gather.7.cloned.1.call-update) | async-done | bytes 7340048 | tf_op jit(solution)/shard_map/all_gather | solution.py:280
  219.2 1.9 all-to-all-done.2.refs_2_.refs_0_.refs_1_
  221.1 1.5 copy-done
  222.6 18.1 %multiply.3 = (f32[896,1408]{1,0:T(8,128)}, f32[896,1408]{1,0:T(8,128)}) custom-call(bf16[16,1792,128]{2,1,0:T(8,128)(2,1)} %bitcast.20, bf16[16,128,512]{2,1,0:T(8,128)(2,1)} %copy-done.1, bf16[16,128,896]{2,1,0:T(8,128)(2,1)} %all_to_all.20.refs_1_, s16[4,240,1408]{2,1,0:T(8,128)(2,1)} %copy-done), custom_call_target="tpu_custom_call" | custom-call | flops 1 | bytes 1 | tf_op jit(solution)/shard_map/multiply/pallas_call | solution.py:151
  240.7 1.5 collective-permute-start.8
  242.2 8.3 %collective-permute-done.8.got_ref = f32[896,1408]{1,0:T(8,128)} collective-permute-done((f32[896,1408]{1,0:T(8,128)}, f32[896,1408]{1,0:T(8,128)}, u32[]{:S(2)}, u32[]{:S(2)}) %collective-permute-start.8) | collective-permute-done | bytes 5046304 | tf_op jit(solution)/shard_map/ppermute | solution.py:287
  250.6 6.2 %code.3 = s16[4,240,1408]{2,1,0:T(8,128)(2,1)} custom-call(f32[896,1408]{1,0:T(8,128)} %get-tuple-element.31.own_ref, f32[896,1408]{1,0:T(8,128)} %collective-permute-done.8.got_ref), custom_call_target="tpu_custom_call" | custom-call | flops 1 | bytes 1 | tf_op jit(solution)/shard_map/code/pallas_call | solution.py:182
  256.8 3.7 %all-to-all-start.3 = ((s16[4,240,1408]{2,1,0:T(8,128)(2,1)}), s16[4,240,1408]{2,1,0:T(8,128)(2,1)S(1)}, u32[]{:S(2)}, u32[]{:S(2)}) async-start(s16[4,240,1408]{2,1,0:T(8,128)(2,1)} %code.3), calls=%async_computation.3 | async-start | bytes 5406720 | tf_op jit(solution)/shard_map/all_to_all | solution.py:290
  260.5 32.5 %all-to-all-done.3.refs_2_.refs_3_ = s16[4,240,1408]{2,1,0:T(8,128)(2,1)S(1)} async-done(((s16[4,240,1408]{2,1,0:T(8,128)(2,1)}), s16[4,240,1408]{2,1,0:T(8,128)(2,1)S(1)}, u32[]{:S(2)}, u32[]{:S(2)}) %all-to-all-start.3) | async-done | bytes 2703392 | tf_op jit(solution)/shard_map/all_to_all | solution.py:290
  293.0 1.5 copy-done.2
  294.5 5.9 %finish.1 = f32[448,1344]{1,0:T(8,128)} custom-call(s32[1]{0:T(128)} %bitcast.odd_ref, s16[4,240,1408]{2,1,0:T(8,128)(2,1)} %copy-done, s16[4,240,1408]{2,1,0:T(8,128)(2,1)} %copy-done, s16[4,240,1408]{2,1,0:T(8,128)(2,1)} %copy-done.2, s16[4,240,1408]{2,1,0:T(8,128)(2,1)} %copy-done.2), custom_call_target="tpu_custom_call" | custom-call | tf_op jit(solution)/shard_map/finish/pallas_call | solution.py:224
  (20 shorter events, 0.0 us)
Async XLA Ops:
  11.0 38.1 %all-to-all-start = ((bf16[16,128,512]{2,1,0:T(8,128)(2,1)}), bf16[16,128,512]{2,1,0:T(8,128)(2,1)S(1)}, u32[]{:S(2)}, u32[]{:S(2)}) async-start(bf16[16,128,512]{2,1,0:T(8,128)(2,1)} %cut_windows.2), calls=%async_computation | async-start | bytes 4194304 | tf_op jit(solution)/shard_map/all_to_all | solution.py:275
  18.6 132.7 %all-gather.5.cloned.1.call-start = ((), (), s32[]{:S(2)}) async-start(), calls=%async_computation.4 | async-start | bytes 7798784 | tf_op jit(solution)/shard_map/all_gather | solution.py:280
  22.7 13.8 %collective-permute-start = (bf16[20,3584]{1,0:T(8,128)(2,1)}, bf16[20,3584]{1,0:T(8,128)(2,1)S(1)}, u32[]{:S(2)}, u32[]{:S(2)}) collective-permute-start(bf16[20,3584]{1,0:T(8,128)(2,1)} %get-tuple-element.20), channel_id=1, source_target_pairs={{0,16},{16,0},{32,48},{48,32},{64,80},{80,64},{96,112},{112,96},{1... | collective-permute-start | bytes 430088 | tf_op jit(solution)/shard_map/ppermute | solution.py:255
  23.8 13.8 %collective-permute-start.1 = (bf16[20,3584]{1,0:T(8,128)(2,1)}, bf16[20,3584]{1,0:T(8,128)(2,1)S(1)}, u32[]{:S(2)}, u32[]{:S(2)}) collective-permute-start(bf16[20,3584]{1,0:T(8,128)(2,1)} %get-tuple-element.21), channel_id=1, source_target_pairs={{0,32},{16,48},{32,64},{48,80},{64,96},{80,112},{96,0},{112,16},{1... | collective-permute-start | bytes 430088 | tf_op jit(solution)/shard_map/ppermute | solution.py:255
  25.3 14.2 %collective-permute-start.2 = (bf16[20,3584]{1,0:T(8,128)(2,1)}, bf16[20,3584]{1,0:T(8,128)(2,1)S(1)}, u32[]{:S(2)}, u32[]{:S(2)}) collective-permute-start(bf16[20,3584]{1,0:T(8,128)(2,1)} %get-tuple-element.22), channel_id=1, source_target_pairs={{0,48},{16,32},{32,80},{48,64},{64,112},{80,96},{96,16},{112,0},{1... | collective-permute-start | bytes 430088 | tf_op jit(solution)/shard_map/ppermute | solution.py:255
  27.1 13.8 %collective-permute-start.3 = (bf16[20,3584]{1,0:T(8,128)(2,1)}, bf16[20,3584]{1,0:T(8,128)(2,1)S(1)}, u32[]{:S(2)}, u32[]{:S(2)}) collective-permute-start(bf16[20,3584]{1,0:T(8,128)(2,1)} %get-tuple-element.23), channel_id=1, source_target_pairs={{0,64},{16,80},{32,96},{48,112},{64,0},{80,16},{96,32},{112,48},{1... | collective-permute-start | bytes 430088 | tf_op jit(solution)/shard_map/ppermute | solution.py:255
  28.8 15.9 %collective-permute-start.4 = (bf16[20,3584]{1,0:T(8,128)(2,1)}, bf16[20,3584]{1,0:T(8,128)(2,1)S(1)}, u32[]{:S(2)}, u32[]{:S(2)}) collective-permute-start(bf16[20,3584]{1,0:T(8,128)(2,1)} %get-tuple-element.24), channel_id=1, source_target_pairs={{0,80},{16,64},{32,112},{48,96},{64,16},{80,0},{96,48},{112,32},{1... | collective-permute-start | bytes 430088 | tf_op jit(solution)/shard_map/ppermute | solution.py:255
  30.4 5.0 %copy-start.10 = (s32[32,1]{0,1:T(1,128)S(1)}, s32[32,1]{0,1:T(1,128)}, u32[]{:S(2)}) copy-start(s32[32,1]{0,1:T(1,128)} %param.6) | copy-start | bytes 388
  30.4 5.7 %copy-start.11 = (s32[1,4]{1,0:T(1,128)S(1)}, s32[1,4]{1,0:T(1,128)}, u32[]{:S(2)}) copy-start(s32[1,4]{1,0:T(1,128)} %param.5) | copy-start | bytes 52
  30.4 7.2 %copy-start.12 = (bf16[20,3584]{1,0:T(8,128)(2,1)S(1)}, bf16[20,3584]{1,0:T(8,128)(2,1)}, u32[]{:S(2)}) copy-start(bf16[20,3584]{1,0:T(8,128)(2,1)} %get-tuple-element.26) | copy-start | bytes 430084
  36.5 12.5 %copy-start.3 = (bf16[20,3584]{1,0:T(8,128)(2,1)}, bf16[20,3584]{1,0:T(8,128)(2,1)S(1)}, u32[]{:S(2)}) copy-start(bf16[20,3584]{1,0:T(8,128)(2,1)S(1)} %collective-permute-done.refs_1_) | copy-start | bytes 430084
  36.5 8.2 %collective-permute-start.5 = (bf16[20,3584]{1,0:T(8,128)(2,1)}, bf16[20,3584]{1,0:T(8,128)(2,1)S(1)}, u32[]{:S(2)}, u32[]{:S(2)}) collective-permute-start(bf16[20,3584]{1,0:T(8,128)(2,1)} %get-tuple-element.25), channel_id=1, source_target_pairs={{0,96},{16,112},{32,0},{48,16},{64,32},{80,48},{96,64},{112,80},{1... | collective-permute-start | bytes 430088 | tf_op jit(solution)/shard_map/ppermute | solution.py:255
  37.6 11.4 %copy-start.4 = (bf16[20,3584]{1,0:T(8,128)(2,1)}, bf16[20,3584]{1,0:T(8,128)(2,1)S(1)}, u32[]{:S(2)}) copy-start(bf16[20,3584]{1,0:T(8,128)(2,1)S(1)} %collective-permute-done.1.refs_2_) | copy-start | bytes 430084
  37.6 9.1 %collective-permute-start.6 = (bf16[20,3584]{1,0:T(8,128)(2,1)S(1)}, bf16[20,3584]{1,0:T(8,128)(2,1)S(1)}, u32[]{:S(2)}, u32[]{:S(2)}) collective-permute-start(bf16[20,3584]{1,0:T(8,128)(2,1)S(1)} %copy-done.12), channel_id=1, source_target_pairs={{0,112},{16,96},{32,16},{48,0},{64,48},{80,32},{96,80},{112,64},{1... | collective-permute-start | bytes 430088 | tf_op jit(solution)/shard_map/ppermute | solution.py:255
  39.5 9.6 %copy-start.5 = (bf16[20,3584]{1,0:T(8,128)(2,1)}, bf16[20,3584]{1,0:T(8,128)(2,1)S(1)}, u32[]{:S(2)}) copy-start(bf16[20,3584]{1,0:T(8,128)(2,1)S(1)} %collective-permute-done.2.refs_3_) | copy-start | bytes 430084
  40.9 8.1 %copy-start.6 = (bf16[20,3584]{1,0:T(8,128)(2,1)}, bf16[20,3584]{1,0:T(8,128)(2,1)S(1)}, u32[]{:S(2)}) copy-start(bf16[20,3584]{1,0:T(8,128)(2,1)S(1)} %collective-permute-done.3.refs_4_) | copy-start | bytes 430084
  44.7 4.4 %copy-start.7 = (bf16[20,3584]{1,0:T(8,128)(2,1)}, bf16[20,3584]{1,0:T(8,128)(2,1)S(1)}, u32[]{:S(2)}) copy-start(bf16[20,3584]{1,0:T(8,128)(2,1)S(1)} %collective-permute-done.4.refs_5_) | copy-start | bytes 430084
  44.7 4.4 %copy-start.8 = (bf16[20,3584]{1,0:T(8,128)(2,1)}, bf16[20,3584]{1,0:T(8,128)(2,1)S(1)}, u32[]{:S(2)}) copy-start(bf16[20,3584]{1,0:T(8,128)(2,1)S(1)} %collective-permute-done.5.refs_6_) | copy-start | bytes 430084
  46.7 2.4 copy-start.9
  49.0 1.3 copy-start.1
  55.5 163.7 %all-gather.7.cloned.1.call-start = ((), (), s32[]{:S(2)}) async-start(), calls=%async_computation.5 | async-start | bytes 7798784 | tf_op jit(solution)/shard_map/all_gather | solution.py:280
  169.4 9.0 %collective-permute-start.7 = (f32[896,1408]{1,0:T(8,128)}, f32[896,1408]{1,0:T(8,128)}, u32[]{:S(2)}, u32[]{:S(2)}) collective-permute-start(f32[896,1408]{1,0:T(8,128)} %get-tuple-element.29), channel_id=1, source_target_pairs={{0,16},{16,0},{32,48},{48,32},{64,80},{80,64},{96,112},{112,96},{1... | collective-permute-start | bytes 15138824 | tf_op jit(solution)/shard_map/ppermute | solution.py:287
  184.7 36.4 %all-to-all-start.2 = ((s16[4,240,1408]{2,1,0:T(8,128)(2,1)}), s16[4,240,1408]{2,1,0:T(8,128)(2,1)S(1)}, u32[]{:S(2)}, u32[]{:S(2)}) async-start(s16[4,240,1408]{2,1,0:T(8,128)(2,1)} %code.2), calls=%async_computation.2 | async-start | bytes 5406720 | tf_op jit(solution)/shard_map/all_to_all | solution.py:290
  221.1 1.5 copy-start
  240.7 9.9 %collective-permute-start.8 = (f32[896,1408]{1,0:T(8,128)}, f32[896,1408]{1,0:T(8,128)}, u32[]{:S(2)}, u32[]{:S(2)}) collective-permute-start(f32[896,1408]{1,0:T(8,128)} %get-tuple-element.32), channel_id=1, source_target_pairs={{0,16},{16,0},{32,48},{48,32},{64,80},{80,64},{96,112},{112,96},{1... | collective-permute-start | bytes 15138824 | tf_op jit(solution)/shard_map/ppermute | solution.py:287
  256.8 36.2 %all-to-all-start.3 = ((s16[4,240,1408]{2,1,0:T(8,128)(2,1)}), s16[4,240,1408]{2,1,0:T(8,128)(2,1)S(1)}, u32[]{:S(2)}, u32[]{:S(2)}) async-start(s16[4,240,1408]{2,1,0:T(8,128)(2,1)} %code.3), calls=%async_computation.3 | async-start | bytes 5406720 | tf_op jit(solution)/shard_map/all_to_all | solution.py:290
  293.0 1.5 copy-start.2
Sparse Core Ops, SparseCore 0:
  55.6 95.6 all-gather.4
  153.4 65.7 all-gather.6

commit v3 on v2

--- a/solution.py
+++ b/solution.py
@@ -125,52 +125,41 @@
     )(core, places, *blocks, *awaited)
 
 
-def multiply(cot, features, *awaited):
+def multiply(cot, features, core, *awaited):
     source_count, rows, tok_count = cot.shape
     width = sum(f.shape[2] for f in features)
-    steps = 4
-    tile = rows // steps
+    steps = 2
+    tile = rows // (2 * steps)
 
     def kernel(cot_ref, *refs):
+        out = refs[-1]
         left = jnp.concatenate([cot_ref[i] for i in range(source_count)], axis=1)
-
-        def dots(out):
-            at = 0
-            for f_ref in refs[: len(features)]:
-                span = f_ref.shape[2]
-                right = f_ref[...].reshape(source_count * tok_count, span)
-                out[:, at : at + span] = jnp.dot(left, right, preferred_element_type=jnp.float32)
-                at += span
-
-        for core, out in enumerate(refs[-2:]):
-
-            @pl.when(pl.program_id(0) // (steps // 2) == core)
-            def _(out=out):
-                dots(out)
+        at = 0
+        for f_ref in refs[: len(features)]:
+            span = f_ref.shape[2]
+            right = f_ref[...].reshape(source_count * tok_count, span)
+            out[:, at : at + span] = jnp.dot(left, right, preferred_element_type=jnp.float32)
+            at += span
 
     return pl.pallas_call(
         kernel,
         grid=(steps,),
-        in_specs=[pl.BlockSpec((source_count, tile, tok_count), lambda i: (0, i, 0))]
+        in_specs=[pl.BlockSpec((source_count, tile, tok_count), lambda i: (0, core * steps + i, 0))]
         + [pl.BlockSpec(f.shape, lambda i: (0, 0, 0)) for f in features]
         + [ANY] * len(awaited),
-        out_specs=[
-            pl.BlockSpec((tile, width), lambda i: (jnp.minimum(i, steps // 2 - 1), 0)),
-            pl.BlockSpec((tile, width), lambda i: (jnp.maximum(i - steps // 2, 0), 0)),
-        ],
-        out_shape=[jax.ShapeDtypeStruct((steps // 2 * tile, width), jnp.float32)] * 2,
-        compiler_params=params(60),
+        out_specs=pl.BlockSpec((tile, width), lambda i: (i, 0)),
+        out_shape=jax.ShapeDtypeStruct((steps * tile, width), jnp.float32),
+        compiler_params=params(24),
         cost_estimate=TINY,
         name="multiply",
     )(cot, *features, *awaited)
 
 
-def code(own, got, *awaited):
+def code(own, got):
     rows, width = own.shape
     m = rows // SIDE
 
-    def kernel(own_ref, got_ref, *refs):
-        out = refs[-1]
+    def kernel(own_ref, got_ref, out):
         total = own_ref[...] + got_ref[...]
         largest = jnp.max(jnp.abs(total), axis=0, keepdims=True)
         level = jnp.ceil(jnp.log2(jnp.maximum(largest, 2.0**-125)) * FINE) + 1.0
@@ -182,54 +171,45 @@
     return pl.pallas_call(
         kernel,
         grid=(SIDE,),
-        in_specs=[pl.BlockSpec((m, width), lambda i: (i, 0))] * 2 + [ANY] * len(awaited),
+        in_specs=[pl.BlockSpec((m, width), lambda i: (i, 0))] * 2,
         out_specs=pl.BlockSpec((1, m + 16, width), lambda i: (i, 0, 0)),
         out_shape=jax.ShapeDtypeStruct((SIDE, m + 16, width), jnp.int16),
-        compiler_params=params(60),
+        compiler_params=params(24),
         cost_estimate=TINY,
         name="code",
-    )(own, got, *awaited)
-
-
-def finish(parts, odd, shift, width):
-    counts = [m // STEP for m in PARTS]
-    firsts = [sum(counts[:p]) for p in range(len(counts))]
-
-    def kernel(odd_ref, *refs):
-        out = refs[-1]
-        for p, (first, count) in enumerate(zip(firsts, counts, strict=True)):
-            rows, levels = refs[2 * p], refs[2 * p + 1]
-
-            @pl.when((pl.program_id(0) >= first) & (pl.program_id(0) < first + count))
-            def _(rows=rows, levels=levels):
-                total = 0.0
-                for z in range(SIDE):
-                    level = levels[z].astype(jnp.int32).astype(jnp.float32)[:1]
-                    scale = jnp.exp2(level * (1.0 / FINE)) * (1.0 / TOP)
-                    total = total + rows[z].astype(jnp.int32).astype(jnp.float32) * scale
-                out[...] = jnp.where(odd_ref[0] == 1, total[:, shift : shift + width], total[:, :width])
-
-    specs, ins = [], []
-    for part, m, first, count in zip(parts, PARTS, firsts, counts, strict=True):
-        window = part.shape[2]
-
-        def where(i, first=first, count=count):
-            return 0, jnp.clip(i - first, 0, count - 1), 0
-
-        def below(i, m=m):
-            return 0, m // 16, 0
-
-        specs += [pl.BlockSpec((SIDE, STEP, window), where), pl.BlockSpec((SIDE, 16, window), below)]
-        ins += [part, part]
-    return pl.pallas_call(
-        kernel,
-        grid=(sum(counts),),
-        in_specs=[SMEM] + specs,
-        out_specs=pl.BlockSpec((STEP, width), lambda i: (i, 0)),
+    )(own, got)
+
+
+def decode(part, p, odd, shift, width, whole):
+    m = PARTS[p]
+    first = sum(PARTS[:p]) // STEP
+    window = part.shape[2]
+
+    def kernel(odd_ref, rows, levels, *refs):
+        total = 0.0
+        for z in range(SIDE):
+            level = levels[z].astype(jnp.int32).astype(jnp.float32)[:1]
+            scale = jnp.exp2(level * (1.0 / FINE)) * (1.0 / TOP)
+            total = total + rows[z].astype(jnp.int32).astype(jnp.float32) * scale
+        refs[-1][...] = jnp.where(odd_ref[0] == 1, total[:, shift : shift + width], total[:, :width])
+
+    held = [] if whole is None else [whole]
+    return pl.pallas_call(
+        kernel,
+        grid=(m // STEP,),
+        in_specs=[
+            SMEM,
+            pl.BlockSpec((SIDE, STEP, window), lambda i: (0, i, 0)),
+            pl.BlockSpec((SIDE, 16, window), lambda i: (0, m // 16, 0)),
+        ]
+        + [ANY] * len(held),
+        out_specs=pl.BlockSpec((STEP, width), lambda i: (first + i, 0)),
         out_shape=jax.ShapeDtypeStruct((sum(PARTS), width), jnp.float32),
-        compiler_params=params(60),
-        name="finish",
-    )(odd, *ins)
+        input_output_aliases={3: 0} if held else {},
+        compiler_params=params(24),
+        cost_estimate=TINY,
+        name="decode",
+    )(odd, part, part, *held)
 
 
 def body(hidden_rows, lengths, balance, cotangent):
@@ -281,17 +261,16 @@
     features = [early, exchange(hold(late, paired[0]))]
 
     planes = [[2 * i + c for i in range(SIDE)] for c in range(2)]
-    coded, came = [], []
-    for cot in gathered:
-        other, own = multiply(cot, features, *came[-1:])
+    whole, came = None, None
+    for p, cot in enumerate(gathered):
+        other = multiply(cot, features, 0, *([] if came is None else [came]))
         got = lax.ppermute(other, "role", along_z(0, 1))
-        coded.append(code(own, got, *came[-2:-1]))
-        came.append(
-            lax.all_to_all(
-                coded[-1], "role", split_axis=0, concat_axis=0, axis_index_groups=planes, tiled=True
-            )
+        own = multiply(cot, features, 1, other)
+        came = lax.all_to_all(
+            code(own, got), "role", split_axis=0, concat_axis=0, axis_index_groups=planes, tiled=True
         )
-    return finish(came, (dev % 2).reshape(1), shift, slice_width)
+        whole = decode(came, p, (dev % 2).reshape(1), shift, slice_width, whole)
+    return whole
 
 
 def solution(mesh):

time: 308 us -> 289 us (0.938)
  Pallas kernels: 72.5 us -> 51.3 us
  local copies, waits for them, and re-layouts: 5.61 us -> 15.8 us
  waiting for transfers between devices: 131 us -> 122 us
    ppermute x2, waiting for transfers between devices: 16.7 us -> 3.45 us  [body(): got = lax.ppermute(other, 'role', along_z(0, 1))]
    pallas_call x2 -> x4, Pallas kernels: 36.2 us -> 25.1 us  [multiply(): pl.pallas_call(kernel, grid=(steps,), in_specs=[pl.BlockSpec((source_coun...]
    unnamed x26 -> x36, local copies, waits for them, and re-layouts: 4.35 us -> 14.6 us
    all_gather x2, waiting for transfers between devices: 69.2 us -> 79.2 us  [body(): lax.all_gather(cot, 'dev', axis=0, tiled=False)]
    pallas_call x2, Pallas kernels: 12.5 us -> 2.81 us  [code(): pl.pallas_call(kernel, grid=(SIDE,), in_specs=[pl.BlockSpec((m, width), l...]
    all_to_all x2, waiting for transfers between devices: 34.4 us -> 29 us  [body(): lax.all_to_all(code(own, got), 'role', split_axis=0, concat_axis=0, axis_...]
  transfers between devices with their start and end apart: 14 -> 14, of which waited for: 10 -> 9; matrix products, arithmetic and copies ran while one was open for 1% -> 1% of each run, Pallas kernels for 11% -> 11%
where the time goes in v3:
time: 289 us; the launch traced here: 288 us
  waiting for transfers between devices  122 us (42%)
  blocking collectives  56 us (19%)
  Pallas kernels  51.3 us (18%)
  starting transfers between devices  28 us (10%)
  local copies, waits for them, and re-layouts  15.8 us (5%)
  between operations  13.7 us (5%)
    all_gather x2, waiting for transfers between devices, body(): lax.all_gather(cot, 'dev', axis=0, tiled=False)  79.2 us
    all_to_all x1, blocking collectives, exchange(): return lax.all_to_all(cut, 'dev', split_axis=0, concat_axis=0, tiled=True)  56 us
    all_to_all x2, waiting for transfers between devices, body(): lax.all_to_all(code(own, got), 'role', split_axis=0, concat_axis=0, axis_...  29 us
    pallas_call x4, Pallas kernels, multiply(): pl.pallas_call(kernel, grid=(steps,), in_specs=[pl.BlockSpec((source_coun...  25.1 us
    unnamed x36, local copies, waits for them, and re-layouts  14.6 us
    ppermute x7, starting transfers between devices, body(): lax.ppermute(block, 'role', along_z(*step))  9.87 us
    pallas_call x2, Pallas kernels, cut_windows(): pl.pallas_call(kernel, grid=(tok_count // tile,), in_specs=[pl.BlockSpec(...  9.38 us
    all_to_all x2, starting transfers between devices, body(): lax.all_to_all(code(own, got), 'role', split_axis=0, concat_axis=0, axis_...  8.75 us
  transfers between devices with their start and end apart: 14, of which 9 were waited for; matrix products, arithmetic and copies ran while one was open for 1% of the time, Pallas kernels for 11%

profile of v3, /device:TPU:1, one launch (start us, length us, event | category | flops | bytes accessed | tf_op | source)
XLA Modules:
  0.0 288.1 jit_solution(12097873558222734205)
XLA Ops:
  6.5 4.4 %cut_windows.2 = bf16[16,128,512]{2,1,0:T(8,128)(2,1)} custom-call(bf16[128,21504]{1,0:T(8,128)(2,1)} %rows_ref.3), custom_call_target="tpu_custom_call" | custom-call | tf_op jit(solution)/shard_map/cut_windows/pallas_call | solution.py:38
  11.0 7.6 %all-to-all-start = ((bf16[16,128,512]{2,1,0:T(8,128)(2,1)}), bf16[16,128,512]{2,1,0:T(8,128)(2,1)S(1)}, u32[]{:S(2)}, u32[]{:S(2)}) async-start(bf16[16,128,512]{2,1,0:T(8,128)(2,1)} %cut_windows.2), calls=%async_computation | async-start | bytes 4194304 | tf_op jit(solution)/shard_map/all_to_all | solution.py:255
  18.6 0.0 all-gather.7.cloned.1.call-start
  18.7 0.6 stack.65.targets_ref
  19.3 3.3 %sort_blocks.1 = (bf16[20,3584]{1,0:T(8,128)(2,1)}, bf16[20,3584]{1,0:T(8,128)(2,1)}, bf16[20,3584]{1,0:T(8,128)(2,1)}, bf16[20,3584]{1,0:T(8,128)(2,1)}, bf16[2...) custom-call(s32[8]{0:T(128)} %stack.65.targets_ref, ...), custom_call_target="tpu_custom_call" | custom-call | tf_op jit(solution)/shard_map/sort_blocks/pallas_call | solution.py:79
  22.6 1.2 collective-permute-start
  23.7 1.4 collective-permute-start.1
  25.2 2.0 collective-permute-start.2
  27.2 1.3 collective-permute-start.3
  28.5 2.0 collective-permute-start.4
  30.5 5.0 %cut_windows.3.refs_9_.value_ref = bf16[16,128,896]{2,1,0:T(8,128)(2,1)} custom-call(bf16[128,21504]{1,0:T(8,128)(2,1)} %rows_ref.3), custom_call_target="tpu_custom_call" | custom-call | tf_op jit(solution)/shard_map/cut_windows/pallas_call | solution.py:38
  35.5 0.1 broadcast_in_dim.16
  35.6 0.1 reshape.99
  35.7 0.1 fusion
  35.7 0.1 reduce_window_sum.11
  35.8 0.2 select_reduce_fusion
  36.0 0.1 broadcast_in_dim.7
  36.1 0.1 mul.56
  36.2 0.1 broadcast_in_dim.6
  36.3 0.1 eq.91
  36.4 0.1 stack.58
  36.5 0.1 broadcast_compare_fusion
  36.5 0.0 collective-permute-done.refs_1_
  36.6 0.9 collective-permute-start.5
  37.5 0.0 collective-permute-done.1.refs_2_
  37.5 1.0 collective-permute-start.6
  38.5 0.6 and_convert_fusion.places_ref
  39.1 0.0 collective-permute-done.2.refs_3_
  39.1 1.5 collective-permute-done.3.refs_4_
  40.6 3.8 %collective-permute-done.4.refs_5_ = bf16[20,3584]{1,0:T(8,128)(2,1)S(1)} collective-permute-done((bf16[20,3584]{1,0:T(8,128)(2,1)}, bf16[20,3584]{1,0:T(8,128)(2,1)S(1)}, u32[]{:S(2)}, u32[]{:S(2)}) %collective-permute-start.4) | collective-permute-done | bytes 143392 | tf_op jit(solution)/shard_map/ppermute | solution.py:235
  44.4 0.0 collective-permute-done.5.refs_6_
  44.4 2.2 collective-permute-done.6.refs_7_
  46.6 2.4 all-to-all-done.refs_8_.refs_0_
  49.1 1.3 copy-done.2
  50.4 5.1 %pair_rows.1 = (bf16[1792,128]{1,0:T(8,128)(2,1)}, bf16[1792,128]{1,0:T(8,128)(2,1)}) custom-call(s32[1]{0:T(128)} %bitcast.1.core_ref, bf16[8,20,128]{2,1,0:T(8,128)(2,1)} %and_convert_fusion.places_ref, bf16[20,3584]{1,0:T(8,128)(2,1)} %get-tuple-element.15.refs_0_, bf16[20,3584]{1,0:T(8,128)(2,1)} %copy-done.8, bf16[20,3584]{1,0:T(8,128)(2,1)} %copy-done.9, ...), custom_call_target="tpu_custom_call" | custom-call | tf_op jit(solution)/shard_map/pair_rows/pallas_call | solution.py:115
  55.5 0.0 all-gather.7.cloned.1.call-update
  55.5 0.0 all-gather.5.cloned.1.call-start
  55.6 0.7 all-gather.5.cloned.1.call-update
  56.3 0.0 copy-start.3
  56.3 56.0 %all_to_all.20.refs_1_ = bf16[16,128,896]{2,1,0:T(8,128)(2,1)} all-to-all(bf16[16,128,896]{2,1,0:T(8,128)(2,1)} %hold.1), channel_id=1, replica_groups=mesh['role'=8,'dev'=16] {'dev'}, dimensions={0} | all-to-all | bytes 7340032 | tf_op jit(solution)/shard_map/all_to_all | solution.py:255
  112.3 39.1 %all-gather.7.cloned.1.call-done = bf16[28672,128]{1,0:T(8,128)(2,1)} async-done(((bf16[1792,128]{1,0:T(8,128)(2,1)}), bf16[28672,128]{1,0:T(8,128)(2,1)}) %all-gather.7.cloned.1.call-update) | async-done | bytes 7340048 | tf_op jit(solution)/shard_map/all_gather | solution.py:260
  151.4 2.0 copy-done
  153.5 3.1 %copy-done.4 = bf16[28672,128]{1,0:T(8,128)(2,1)S(1)} copy-done((bf16[28672,128]{1,0:T(8,128)(2,1)S(1)}, bf16[28672,128]{1,0:T(8,128)(2,1)}, u32[]{:S(2)}) %copy-start.4) | copy-done | bytes 7340056
  156.6 6.3 %multiply.4.refs_2_ = f32[896,1408]{1,0:T(8,128)S(1)} custom-call(bf16[16,1792,128]{2,1,0:T(8,128)(2,1)S(1)} %bitcast.20, bf16[16,128,512]{2,1,0:T(8,128)(2,1)S(1)} %copy-done.3, bf16[16,128,896]{2,1,0:T(8,128)(2,1)S(1)} %copy-done), custom_call_target="tpu_custom_call" | custom-call | flops 1 | bytes 1 | tf_op jit(solution)/shard_map/multiply/pallas_call | solution.py:144
  162.8 0.8 collective-permute-start.7
  163.6 6.3 %multiply.5.own_ref = f32[896,1408]{1,0:T(8,128)S(1)} custom-call(bf16[16,1792,128]{2,1,0:T(8,128)(2,1)S(1)} %bitcast.21, bf16[16,128,512]{2,1,0:T(8,128)(2,1)S(1)} %copy-done.3, bf16[16,128,896]{2,1,0:T(8,128)(2,1)S(1)} %copy-done, f32[896,1408]{1,0:T(8,128)S(1)} %multiply.4.refs_2_), custom_call_target="tpu_custom_call" | custom-call | flops 1 | bytes 1 | tf_op jit(solution)/shard_map/multiply/pallas_call | solution.py:144
  169.9 1.7 collective-permute-done.7.got_ref
  171.6 1.4 code.2
  173.0 1.6 copy-done.7
  174.6 4.6 %all-to-all-start.2 = ((s16[4,240,1408]{2,1,0:T(8,128)(2,1)}), s16[4,240,1408]{2,1,0:T(8,128)(2,1)}, u32[]{:S(2)}, u32[]{:S(2)}) async-start(s16[4,240,1408]{2,1,0:T(8,128)(2,1)} %copy-done.7), calls=%async_computation.2 | async-start | bytes 5406720 | tf_op jit(solution)/shard_map/all_to_all | solution.py:269
  179.2 40.1 %all-gather.5.cloned.1.call-done = bf16[28672,128]{1,0:T(8,128)(2,1)} async-done(((bf16[1792,128]{1,0:T(8,128)(2,1)}), bf16[28672,128]{1,0:T(8,128)(2,1)}) %all-gather.5.cloned.1.call-update) | async-done | bytes 7340048 | tf_op jit(solution)/shard_map/all_gather | solution.py:260
  219.3 0.0 all-to-all-done.2.refs_2_.rows.levels
  219.3 2.0 copy-done.1
  221.4 3.1 %copy-done.5 = bf16[28672,128]{1,0:T(8,128)(2,1)S(1)} copy-done((bf16[28672,128]{1,0:T(8,128)(2,1)S(1)}, bf16[28672,128]{1,0:T(8,128)(2,1)}, u32[]{:S(2)}) %copy-start.5) | copy-done | bytes 7340056
  224.5 6.3 %multiply.6.refs_2_ = f32[896,1408]{1,0:T(8,128)S(1)} custom-call(bf16[16,1792,128]{2,1,0:T(8,128)(2,1)S(1)} %bitcast.22, bf16[16,128,512]{2,1,0:T(8,128)(2,1)S(1)} %copy-done.3, bf16[16,128,896]{2,1,0:T(8,128)(2,1)S(1)} %copy-done.1, s16[4,240,1408]{2,1,0:T(8,128)(2,1)} %all-to-all-done.2.refs_2_.rows.levels), custom_call_target="tpu_custom_call" | custom-call | flops 1 | bytes 1 | tf_op jit(solution)/shard_map/multiply/pallas_call | solution.py:144
  230.7 0.9 collective-permute-start.8
  231.7 6.3 %multiply.7.own_ref = f32[896,1408]{1,0:T(8,128)S(1)} custom-call(bf16[16,1792,128]{2,1,0:T(8,128)(2,1)S(1)} %bitcast.23, bf16[16,128,512]{2,1,0:T(8,128)(2,1)S(1)} %copy-done.3, bf16[16,128,896]{2,1,0:T(8,128)(2,1)S(1)} %copy-done.1, f32[896,1408]{1,0:T(8,128)S(1)} %multiply.6.refs_2_), custom_call_target="tpu_custom_call" | custom-call | flops 1 | bytes 1 | tf_op jit(solution)/shard_map/multiply/pallas_call | solution.py:144
  238.0 1.7 collective-permute-done.8.got_ref
  239.7 1.4 code.3
  241.1 1.5 copy-done.6
  242.6 4.1 %all-to-all-start.3 = ((s16[4,240,1408]{2,1,0:T(8,128)(2,1)}), s16[4,240,1408]{2,1,0:T(8,128)(2,1)S(1)}, u32[]{:S(2)}, u32[]{:S(2)}) async-start(s16[4,240,1408]{2,1,0:T(8,128)(2,1)} %copy-done.6), calls=%async_computation.3 | async-start | bytes 5406720 | tf_op jit(solution)/shard_map/all_to_all | solution.py:269
  246.7 3.3 %decode.2.refs_0_ = f32[448,1344]{1,0:T(8,128)} custom-call(s32[1]{0:T(128)} %bitcast.odd_ref, s16[4,240,1408]{2,1,0:T(8,128)(2,1)} %all-to-all-done.2.refs_2_.rows.levels, s16[4,240,1408]{2,1,0:T(8,128)(2,1)} %all-to-all-done.2.refs_2_.rows.levels), custom_call_target="tpu_custom_call" | custom-call | flops 1 | bytes 1 | tf_op jit(solution)/shard_map/decode/pallas_call | solution.py:197
  250.1 29.0 %all-to-all-done.3.rows.levels = s16[4,240,1408]{2,1,0:T(8,128)(2,1)S(1)} async-done(((s16[4,240,1408]{2,1,0:T(8,128)(2,1)}), s16[4,240,1408]{2,1,0:T(8,128)(2,1)S(1)}, u32[]{:S(2)}, u32[]{:S(2)}) %all-to-all-start.3) | async-done | bytes 2703392 | tf_op jit(solution)/shard_map/all_to_all | solution.py:269
  279.0 2.3 decode.3
  (33 shorter events, 0.1 us)
Async XLA Ops:
  11.0 38.1 %all-to-all-start = ((bf16[16,128,512]{2,1,0:T(8,128)(2,1)}), bf16[16,128,512]{2,1,0:T(8,128)(2,1)S(1)}, u32[]{:S(2)}, u32[]{:S(2)}) async-start(bf16[16,128,512]{2,1,0:T(8,128)(2,1)} %cut_windows.2), calls=%async_computation | async-start | bytes 4194304 | tf_op jit(solution)/shard_map/all_to_all | solution.py:255
  18.6 132.9 %all-gather.7.cloned.1.call-start = ((), (), s32[]{:S(2)}) async-start(), calls=%async_computation.5 | async-start | bytes 7798784 | tf_op jit(solution)/shard_map/all_gather | solution.py:260
  22.6 14.0 %collective-permute-start = (bf16[20,3584]{1,0:T(8,128)(2,1)}, bf16[20,3584]{1,0:T(8,128)(2,1)S(1)}, u32[]{:S(2)}, u32[]{:S(2)}) collective-permute-start(bf16[20,3584]{1,0:T(8,128)(2,1)} %get-tuple-element.16), channel_id=1, source_target_pairs={{0,16},{16,0},{32,48},{48,32},{64,80},{80,64},{96,112},{112,96},{1... | collective-permute-start | bytes 430088 | tf_op jit(solution)/shard_map/ppermute | solution.py:235
  23.7 13.8 %collective-permute-start.1 = (bf16[20,3584]{1,0:T(8,128)(2,1)}, bf16[20,3584]{1,0:T(8,128)(2,1)S(1)}, u32[]{:S(2)}, u32[]{:S(2)}) collective-permute-start(bf16[20,3584]{1,0:T(8,128)(2,1)} %get-tuple-element.17), channel_id=1, source_target_pairs={{0,32},{16,48},{32,64},{48,80},{64,96},{80,112},{96,0},{112,16},{1... | collective-permute-start | bytes 430088 | tf_op jit(solution)/shard_map/ppermute | solution.py:235
  25.2 13.9 %collective-permute-start.2 = (bf16[20,3584]{1,0:T(8,128)(2,1)}, bf16[20,3584]{1,0:T(8,128)(2,1)S(1)}, u32[]{:S(2)}, u32[]{:S(2)}) collective-permute-start(bf16[20,3584]{1,0:T(8,128)(2,1)} %get-tuple-element.18), channel_id=1, source_target_pairs={{0,48},{16,32},{32,80},{48,64},{64,112},{80,96},{96,16},{112,0},{1... | collective-permute-start | bytes 430088 | tf_op jit(solution)/shard_map/ppermute | solution.py:235
  27.2 13.5 %collective-permute-start.3 = (bf16[20,3584]{1,0:T(8,128)(2,1)}, bf16[20,3584]{1,0:T(8,128)(2,1)S(1)}, u32[]{:S(2)}, u32[]{:S(2)}) collective-permute-start(bf16[20,3584]{1,0:T(8,128)(2,1)} %get-tuple-element.19), channel_id=1, source_target_pairs={{0,64},{16,80},{32,96},{48,112},{64,0},{80,16},{96,32},{112,48},{1... | collective-permute-start | bytes 430088 | tf_op jit(solution)/shard_map/ppermute | solution.py:235
  28.5 15.9 %collective-permute-start.4 = (bf16[20,3584]{1,0:T(8,128)(2,1)}, bf16[20,3584]{1,0:T(8,128)(2,1)S(1)}, u32[]{:S(2)}, u32[]{:S(2)}) collective-permute-start(bf16[20,3584]{1,0:T(8,128)(2,1)} %get-tuple-element.20), channel_id=1, source_target_pairs={{0,80},{16,64},{32,112},{48,96},{64,16},{80,0},{96,48},{112,32},{1... | collective-permute-start | bytes 430088 | tf_op jit(solution)/shard_map/ppermute | solution.py:235
  30.5 5.0 %copy-start.16 = (s32[1,4]{1,0:T(1,128)S(1)}, s32[1,4]{1,0:T(1,128)}, u32[]{:S(2)}) copy-start(s32[1,4]{1,0:T(1,128)} %param.5) | copy-start | bytes 52
  30.5 5.1 %copy-start.15 = (s32[32,1]{0,1:T(1,128)S(1)}, s32[32,1]{0,1:T(1,128)}, u32[]{:S(2)}) copy-start(s32[32,1]{0,1:T(1,128)} %param.6) | copy-start | bytes 388
  30.5 6.9 %copy-start.17 = (bf16[20,3584]{1,0:T(8,128)(2,1)S(1)}, bf16[20,3584]{1,0:T(8,128)(2,1)}, u32[]{:S(2)}) copy-start(bf16[20,3584]{1,0:T(8,128)(2,1)} %get-tuple-element.22) | copy-start | bytes 430084
  36.6 12.5 %copy-start.8 = (bf16[20,3584]{1,0:T(8,128)(2,1)}, bf16[20,3584]{1,0:T(8,128)(2,1)S(1)}, u32[]{:S(2)}) copy-start(bf16[20,3584]{1,0:T(8,128)(2,1)S(1)} %collective-permute-done.refs_1_) | copy-start | bytes 430084
  36.6 7.8 %collective-permute-start.5 = (bf16[20,3584]{1,0:T(8,128)(2,1)}, bf16[20,3584]{1,0:T(8,128)(2,1)S(1)}, u32[]{:S(2)}, u32[]{:S(2)}) collective-permute-start(bf16[20,3584]{1,0:T(8,128)(2,1)} %get-tuple-element.21), channel_id=1, source_target_pairs={{0,96},{16,112},{32,0},{48,16},{64,32},{80,48},{96,64},{112,80},{1... | collective-permute-start | bytes 430088 | tf_op jit(solution)/shard_map/ppermute | solution.py:235
  37.5 11.6 %copy-start.9 = (bf16[20,3584]{1,0:T(8,128)(2,1)}, bf16[20,3584]{1,0:T(8,128)(2,1)S(1)}, u32[]{:S(2)}) copy-start(bf16[20,3584]{1,0:T(8,128)(2,1)S(1)} %collective-permute-done.1.refs_2_) | copy-start | bytes 430084
  37.5 9.1 %collective-permute-start.6 = (bf16[20,3584]{1,0:T(8,128)(2,1)S(1)}, bf16[20,3584]{1,0:T(8,128)(2,1)S(1)}, u32[]{:S(2)}, u32[]{:S(2)}) collective-permute-start(bf16[20,3584]{1,0:T(8,128)(2,1)S(1)} %copy-done.17), channel_id=1, source_target_pairs={{0,112},{16,96},{32,16},{48,0},{64,48},{80,32},{96,80},{112,64},{1... | collective-permute-start | bytes 430088 | tf_op jit(solution)/shard_map/ppermute | solution.py:235
  39.1 9.9 %copy-start.10 = (bf16[20,3584]{1,0:T(8,128)(2,1)}, bf16[20,3584]{1,0:T(8,128)(2,1)S(1)}, u32[]{:S(2)}) copy-start(bf16[20,3584]{1,0:T(8,128)(2,1)S(1)} %collective-permute-done.2.refs_3_) | copy-start | bytes 430084
  40.6 8.4 %copy-start.11 = (bf16[20,3584]{1,0:T(8,128)(2,1)}, bf16[20,3584]{1,0:T(8,128)(2,1)S(1)}, u32[]{:S(2)}) copy-start(bf16[20,3584]{1,0:T(8,128)(2,1)S(1)} %collective-permute-done.3.refs_4_) | copy-start | bytes 430084
  44.4 4.7 %copy-start.12 = (bf16[20,3584]{1,0:T(8,128)(2,1)}, bf16[20,3584]{1,0:T(8,128)(2,1)S(1)}, u32[]{:S(2)}) copy-start(bf16[20,3584]{1,0:T(8,128)(2,1)S(1)} %collective-permute-done.4.refs_5_) | copy-start | bytes 430084
  44.4 4.7 %copy-start.13 = (bf16[20,3584]{1,0:T(8,128)(2,1)}, bf16[20,3584]{1,0:T(8,128)(2,1)S(1)}, u32[]{:S(2)}) copy-start(bf16[20,3584]{1,0:T(8,128)(2,1)S(1)} %collective-permute-done.5.refs_6_) | copy-start | bytes 430084
  46.6 2.4 copy-start.14
  49.0 1.3 copy-start.2
  55.5 163.8 %all-gather.5.cloned.1.call-start = ((), (), s32[]{:S(2)}) async-start(), calls=%async_computation.4 | async-start | bytes 7798784 | tf_op jit(solution)/shard_map/all_gather | solution.py:260
  56.3 95.2 %copy-start.3 = (bf16[16,128,512]{2,1,0:T(8,128)(2,1)S(1)}, bf16[16,128,512]{2,1,0:T(8,128)(2,1)}, u32[]{:S(2)}) copy-start(bf16[16,128,512]{2,1,0:T(8,128)(2,1)} %copy-done.2) | copy-start | bytes 6291460
  151.4 2.0 copy-start
  153.5 3.1 %copy-start.4 = (bf16[28672,128]{1,0:T(8,128)(2,1)S(1)}, bf16[28672,128]{1,0:T(8,128)(2,1)}, u32[]{:S(2)}) copy-start(bf16[28672,128]{1,0:T(8,128)(2,1)} %all-gather.7.cloned.1.call-done) | copy-start | bytes 22020100
  162.8 8.8 %collective-permute-start.7 = (f32[896,1408]{1,0:T(8,128)S(1)}, f32[896,1408]{1,0:T(8,128)S(1)}, u32[]{:S(2)}, u32[]{:S(2)}) collective-permute-start(f32[896,1408]{1,0:T(8,128)S(1)} %multiply.4.refs_2_), channel_id=1, source_target_pairs={{0,16},{16,0},{32,48},{48,32},{64,80},{80,64},{96,112},{112,96},{1... | collective-permute-start | bytes 15138824 | tf_op jit(solution)/shard_map/ppermute | solution.py:267
  173.0 1.6 copy-start.7
  174.6 44.8 %all-to-all-start.2 = ((s16[4,240,1408]{2,1,0:T(8,128)(2,1)}), s16[4,240,1408]{2,1,0:T(8,128)(2,1)}, u32[]{:S(2)}, u32[]{:S(2)}) async-start(s16[4,240,1408]{2,1,0:T(8,128)(2,1)} %copy-done.7), calls=%async_computation.2 | async-start | bytes 5406720 | tf_op jit(solution)/shard_map/all_to_all | solution.py:269
  219.3 2.0 copy-start.1
  221.4 3.1 %copy-start.5 = (bf16[28672,128]{1,0:T(8,128)(2,1)S(1)}, bf16[28672,128]{1,0:T(8,128)(2,1)}, u32[]{:S(2)}) copy-start(bf16[28672,128]{1,0:T(8,128)(2,1)} %all-gather.5.cloned.1.call-done) | copy-start | bytes 22020100
  230.7 8.9 %collective-permute-start.8 = (f32[896,1408]{1,0:T(8,128)S(1)}, f32[896,1408]{1,0:T(8,128)S(1)}, u32[]{:S(2)}, u32[]{:S(2)}) collective-permute-start(f32[896,1408]{1,0:T(8,128)S(1)} %multiply.6.refs_2_), channel_id=1, source_target_pairs={{0,16},{16,0},{32,48},{48,32},{64,80},{80,64},{96,112},{112,96},{1... | collective-permute-start | bytes 15138824 | tf_op jit(solution)/shard_map/ppermute | solution.py:267
  241.1 1.5 copy-start.6
  242.6 36.4 %all-to-all-start.3 = ((s16[4,240,1408]{2,1,0:T(8,128)(2,1)}), s16[4,240,1408]{2,1,0:T(8,128)(2,1)S(1)}, u32[]{:S(2)}, u32[]{:S(2)}) async-start(s16[4,240,1408]{2,1,0:T(8,128)(2,1)} %copy-done.6), calls=%async_computation.3 | async-start | bytes 5406720 | tf_op jit(solution)/shard_map/all_to_all | solution.py:269
Sparse Core Ops, SparseCore 0:
  55.6 95.7 all-gather.6
  153.6 65.7 all-gather.4

commit v4 on v3

--- a/solution.py
+++ b/solution.py
@@ -5,12 +5,13 @@
 from jax.experimental.pallas import tpu as pltpu
 from jax.sharding import PartitionSpec as P
 
-PARTS = (224, 224)
-STEP = 112
+PARTS = (256, 192)
+STEP = 64
 SPANS = (512, 896)
 FINE = 256.0
 TOP = 32767.0
 SIDE = 4
+PLACE = 32
 VMEM = pl.BlockSpec(memory_space=pltpu.VMEM)
 SMEM = pl.BlockSpec(memory_space=pltpu.SMEM)
 ANY = pl.BlockSpec(memory_space=pl.ANY)
@@ -93,16 +94,22 @@
     share = width // count
 
     def kernel(core_ref, places_ref, *refs):
-        ins, outs = refs[:count], refs[-len(PARTS) :]
+        ins, outs = refs[:count], refs[-1 - len(PARTS) : -1]
         z = pl.program_id(0)
-        total = jnp.zeros((2 * share, tok_count), jnp.float32)
+        stacked = refs[-1]
+
+        @pl.when(z == 0)
+        def _():
+            stacked[...] = jnp.zeros_like(stacked)
+
         for j in range(count):
-            total += lax.dot_general(
-                ins[j][...],
-                places_ref[j],
-                (((0,), (0,)), ((), ())),
-                preferred_element_type=jnp.float32,
-            )
+            stacked[j * PLACE : j * PLACE + block] = ins[j][...]
+        total = lax.dot_general(
+            stacked[...],
+            places_ref[...].reshape(count * PLACE, tok_count),
+            (((0,), (0,)), ((), ())),
+            preferred_element_type=jnp.float32,
+        )
         total = total.astype(jnp.bfloat16)
         for q in range(2):
             own = jnp.where(core_ref[0] == q, 1, 0)
@@ -115,11 +122,12 @@
     return pl.pallas_call(
         kernel,
         grid=(SIDE,),
-        in_specs=[SMEM, pl.BlockSpec((count, block, tok_count), lambda i: (0, 0, 0))]
+        in_specs=[SMEM, pl.BlockSpec((count, PLACE, tok_count), lambda i: (0, 0, 0))]
         + [pl.BlockSpec((block, 2 * share), lambda i: (0, i))] * count
         + [ANY] * len(awaited),
         out_specs=[pl.BlockSpec((count * m, tok_count), lambda i: (0, 0)) for m in PARTS],
         out_shape=[jax.ShapeDtypeStruct((count * m, tok_count), jnp.bfloat16) for m in PARTS],
+        scratch_shapes=[pltpu.VMEM((count * PLACE, 2 * share), jnp.bfloat16)],
         compiler_params=params(60),
         name="pair_rows",
     )(core, places, *blocks, *awaited)
@@ -244,7 +252,7 @@
     row_of_token = jnp.repeat(block_rank, block_rows) * block_rows + token % block_rows
     group_of_token = jnp.repeat(groups, block_rows)
     keeping = token % slot_len < jnp.repeat(lengths[0], slot_len)
-    rows = jnp.arange(pair_count, dtype=jnp.int32)
+    rows = jnp.arange(PLACE, dtype=jnp.int32)
     places = (
         (behind[:, None, None] == group_of_token[None, None, :])
         & (rows[None, :, None] == row_of_token[None, None, :])

time: 289 us -> 286 us (0.990)
  waiting for transfers between devices: 122 us -> 118 us
  transfers between devices with their start and end apart: 14 -> 14, of which waited for: 9 -> 10; matrix products, arithmetic and copies ran while one was open for 1% -> 1% of each run, Pallas kernels for 11% -> 12%
where the time goes in v4:
time: 286 us; the launch traced here: 285 us
  waiting for transfers between devices  118 us (41%)
  blocking collectives  56.9 us (20%)
  Pallas kernels  51.6 us (18%)
  starting transfers between devices  28 us (10%)
  local copies, waits for them, and re-layouts  15.7 us (5%)
  between operations  13.8 us (5%)
    all_gather x2, waiting for transfers between devices, body(): lax.all_gather(cot, 'dev', axis=0, tiled=False)  76.4 us
    all_to_all x1, blocking collectives, exchange(): return lax.all_to_all(cut, 'dev', split_axis=0, concat_axis=0, tiled=True)  56.9 us
    all_to_all x2, waiting for transfers between devices, body(): lax.all_to_all(code(own, got), 'role', split_axis=0, concat_axis=0, axis_...  27.7 us
    pallas_call x4, Pallas kernels, multiply(): pl.pallas_call(kernel, grid=(steps,), in_specs=[pl.BlockSpec((source_coun...  25.1 us
    unnamed x36, local copies, waits for them, and re-layouts  14.6 us
    ppermute x7, starting transfers between devices, body(): lax.ppermute(block, 'role', along_z(*step))  9.87 us
    pallas_call x2, Pallas kernels, cut_windows(): pl.pallas_call(kernel, grid=(tok_count // tile,), in_specs=[pl.BlockSpec(...  9.38 us
    all_to_all x2, starting transfers between devices, body(): lax.all_to_all(code(own, got), 'role', split_axis=0, concat_axis=0, axis_...  8.28 us
  transfers between devices with their start and end apart: 14, of which 10 were waited for; matrix products, arithmetic and copies ran while one was open for 1% of the time, Pallas kernels for 12%

profile of v4, /device:TPU:1, one launch (start us, length us, event | category | flops | bytes accessed | tf_op | source)
XLA Modules:
  0.0 285.2 jit_solution(9348726802967666190)
XLA Ops:
  6.5 4.4 %cut_windows.2 = bf16[16,128,512]{2,1,0:T(8,128)(2,1)} custom-call(bf16[128,21504]{1,0:T(8,128)(2,1)} %rows_ref.3), custom_call_target="tpu_custom_call" | custom-call | tf_op jit(solution)/shard_map/cut_windows/pallas_call | solution.py:39
  11.0 7.6 %all-to-all-start = ((bf16[16,128,512]{2,1,0:T(8,128)(2,1)}), bf16[16,128,512]{2,1,0:T(8,128)(2,1)S(1)}, u32[]{:S(2)}, u32[]{:S(2)}) async-start(bf16[16,128,512]{2,1,0:T(8,128)(2,1)} %cut_windows.2), calls=%async_computation | async-start | bytes 4194304 | tf_op jit(solution)/shard_map/all_to_all | solution.py:263
  18.6 0.0 all-gather.7.cloned.1.call-start
  18.7 0.6 stack.65.targets_ref
  19.3 3.3 %sort_blocks.1 = (bf16[20,3584]{1,0:T(8,128)(2,1)}, bf16[20,3584]{1,0:T(8,128)(2,1)}, bf16[20,3584]{1,0:T(8,128)(2,1)}, bf16[20,3584]{1,0:T(8,128)(2,1)}, bf16[2...) custom-call(s32[8]{0:T(128)} %stack.65.targets_ref, ...), custom_call_target="tpu_custom_call" | custom-call | tf_op jit(solution)/shard_map/sort_blocks/pallas_call | solution.py:80
  22.6 1.2 collective-permute-start
  23.7 1.4 collective-permute-start.1
  25.2 2.0 collective-permute-start.2
  27.2 1.3 collective-permute-start.3
  28.5 2.0 collective-permute-start.4
  30.5 5.0 %cut_windows.3.refs_9_.value_ref = bf16[16,128,896]{2,1,0:T(8,128)(2,1)} custom-call(bf16[128,21504]{1,0:T(8,128)(2,1)} %rows_ref.3), custom_call_target="tpu_custom_call" | custom-call | tf_op jit(solution)/shard_map/cut_windows/pallas_call | solution.py:39
  35.5 0.1 broadcast_in_dim.6
  35.6 0.1 eq.91
  35.7 0.1 fusion
  35.8 0.1 reduce_window_sum.11
  35.8 0.2 select_reduce_fusion
  36.0 0.1 broadcast_in_dim.7
  36.1 0.1 mul.56
  36.2 0.1 broadcast_in_dim.16
  36.3 0.1 reshape.99
  36.4 0.1 stack.58
  36.5 0.1 broadcast_compare_fusion
  36.6 0.0 collective-permute-done.refs_1_
  36.6 0.9 collective-permute-start.5
  37.5 0.0 collective-permute-done.1.refs_2_
  37.5 1.0 collective-permute-start.6
  38.5 0.6 and_convert_fusion.places_ref
  39.1 0.0 collective-permute-done.2.refs_3_
  39.1 1.5 collective-permute-done.3.refs_4_
  40.6 3.8 %collective-permute-done.4.refs_5_ = bf16[20,3584]{1,0:T(8,128)(2,1)S(1)} collective-permute-done((bf16[20,3584]{1,0:T(8,128)(2,1)}, bf16[20,3584]{1,0:T(8,128)(2,1)S(1)}, u32[]{:S(2)}, u32[]{:S(2)}) %collective-permute-start.4) | collective-permute-done | bytes 143392 | tf_op jit(solution)/shard_map/ppermute | solution.py:243
  44.4 0.0 collective-permute-done.5.refs_6_
  44.4 2.2 collective-permute-done.6.refs_7_
  46.6 2.4 all-to-all-done.refs_8_.refs_0_
  49.1 1.3 copy-done.2
  50.4 4.1 %pair_rows.1 = (bf16[2048,128]{1,0:T(8,128)(2,1)}, bf16[1536,128]{1,0:T(8,128)(2,1)}) custom-call(s32[1]{0:T(128)} %bitcast.1.core_ref, bf16[8,32,128]{2,1,0:T(8,128)(2,1)} %and_convert_fusion.places_ref, bf16[20,3584]{1,0:T(8,128)(2,1)} %get-tuple-element.15.refs_0_, bf16[20,3584]{1,0:T(8,128)(2,1)} %copy-done.8, bf16[20,3584]{1,0:T(8,128)(2,1)} %copy-done.9, ...), custom_call_target="tpu_custom_call" | custom-call | tf_op jit(solution)/shard_map/pair_rows/pallas_call | solution.py:122
  54.4 0.0 all-gather.7.cloned.1.call-update
  54.5 0.0 all-gather.5.cloned.1.call-start
  54.5 0.7 all-gather.5.cloned.1.call-update
  55.2 0.0 copy-start.3
  55.2 56.9 %all_to_all.20.refs_1_ = bf16[16,128,896]{2,1,0:T(8,128)(2,1)} all-to-all(bf16[16,128,896]{2,1,0:T(8,128)(2,1)} %hold.1), channel_id=1, replica_groups=mesh['role'=8,'dev'=16] {'dev'}, dimensions={0} | all-to-all | bytes 7340032 | tf_op jit(solution)/shard_map/all_to_all | solution.py:263
  112.2 43.5 %all-gather.7.cloned.1.call-done = bf16[32768,128]{1,0:T(8,128)(2,1)} async-done(((bf16[2048,128]{1,0:T(8,128)(2,1)}), bf16[32768,128]{1,0:T(8,128)(2,1)}) %all-gather.7.cloned.1.call-update) | async-done | bytes 8388624 | tf_op jit(solution)/shard_map/all_gather | solution.py:268
  155.6 2.0 copy-done
  157.7 3.4 %copy-done.4 = bf16[32768,128]{1,0:T(8,128)(2,1)S(1)} copy-done((bf16[32768,128]{1,0:T(8,128)(2,1)S(1)}, bf16[32768,128]{1,0:T(8,128)(2,1)}, u32[]{:S(2)}) %copy-start.4) | copy-done | bytes 8388632
  161.0 7.1 %multiply.4.refs_2_ = f32[1024,1408]{1,0:T(8,128)S(1)} custom-call(bf16[16,2048,128]{2,1,0:T(8,128)(2,1)S(1)} %bitcast.20, bf16[16,128,512]{2,1,0:T(8,128)(2,1)S(1)} %copy-done.3, bf16[16,128,896]{2,1,0:T(8,128)(2,1)S(1)} %copy-done), custom_call_target="tpu_custom_call" | custom-call | flops 1 | bytes 1 | tf_op jit(solution)/shard_map/multiply/pallas_call | solution.py:152
  168.2 0.8 collective-permute-start.7
  168.9 7.1 %multiply.5.own_ref = f32[1024,1408]{1,0:T(8,128)S(1)} custom-call(bf16[16,2048,128]{2,1,0:T(8,128)(2,1)S(1)} %bitcast.21, bf16[16,128,512]{2,1,0:T(8,128)(2,1)S(1)} %copy-done.3, bf16[16,128,896]{2,1,0:T(8,128)(2,1)S(1)} %copy-done, f32[1024,1408]{1,0:T(8,128)S(1)} %multiply.4.refs_2_), custom_call_target="tpu_custom_call" | custom-call | flops 1 | bytes 1 | tf_op jit(solution)/shard_map/multiply/pallas_call | solution.py:152
  176.0 1.9 collective-permute-done.7.got_ref
  178.0 1.6 code.2
  179.6 1.6 copy-done.6
  181.2 4.7 %all-to-all-start.2 = ((s16[4,272,1408]{2,1,0:T(8,128)(2,1)}), s16[4,272,1408]{2,1,0:T(8,128)(2,1)}, u32[]{:S(2)}, u32[]{:S(2)}) async-start(s16[4,272,1408]{2,1,0:T(8,128)(2,1)} %copy-done.6), calls=%async_computation.2 | async-start | bytes 6127616 | tf_op jit(solution)/shard_map/all_to_all | solution.py:277
  185.8 32.9 %all-gather.5.cloned.1.call-done = bf16[24576,128]{1,0:T(8,128)(2,1)} async-done(((bf16[1536,128]{1,0:T(8,128)(2,1)}), bf16[24576,128]{1,0:T(8,128)(2,1)}) %all-gather.5.cloned.1.call-update) | async-done | bytes 6291472 | tf_op jit(solution)/shard_map/all_gather | solution.py:268
  218.7 3.6 %all-to-all-done.2.refs_2_.rows.levels = s16[4,272,1408]{2,1,0:T(8,128)(2,1)} async-done(((s16[4,272,1408]{2,1,0:T(8,128)(2,1)}), s16[4,272,1408]{2,1,0:T(8,128)(2,1)}, u32[]{:S(2)}, u32[]{:S(2)}) %all-to-all-start.2) | async-done | bytes 3063840 | tf_op jit(solution)/shard_map/all_to_all | solution.py:277
  222.3 2.0 copy-done.1
  224.4 2.8 copy-done.5
  227.2 5.4 %multiply.6.refs_2_ = f32[768,1408]{1,0:T(8,128)S(1)} custom-call(bf16[16,1536,128]{2,1,0:T(8,128)(2,1)S(1)} %bitcast.22, bf16[16,128,512]{2,1,0:T(8,128)(2,1)S(1)} %copy-done.3, bf16[16,128,896]{2,1,0:T(8,128)(2,1)S(1)} %copy-done.1, s16[4,272,1408]{2,1,0:T(8,128)(2,1)} %all-to-all-done.2.refs_2_.rows.levels), custom_call_target="tpu_custom_call" | custom-call | flops 1 | bytes 1 | tf_op jit(solution)/shard_map/multiply/pallas_call | solution.py:152
  232.6 1.5 collective-permute-start.8
  234.1 5.4 %multiply.7.own_ref = f32[768,1408]{1,0:T(8,128)S(1)} custom-call(bf16[16,1536,128]{2,1,0:T(8,128)(2,1)S(1)} %bitcast.23, bf16[16,128,512]{2,1,0:T(8,128)(2,1)S(1)} %copy-done.3, bf16[16,128,896]{2,1,0:T(8,128)(2,1)S(1)} %copy-done.1, f32[768,1408]{1,0:T(8,128)S(1)} %multiply.6.refs_2_), custom_call_target="tpu_custom_call" | custom-call | flops 1 | bytes 1 | tf_op jit(solution)/shard_map/multiply/pallas_call | solution.py:152
  239.5 1.5 collective-permute-done.8.got_ref
  241.0 1.2 code.3
  242.2 1.4 copy-done.7
  243.6 3.6 %all-to-all-start.3 = ((s16[4,208,1408]{2,1,0:T(8,128)(2,1)}), s16[4,208,1408]{2,1,0:T(8,128)(2,1)S(1)}, u32[]{:S(2)}, u32[]{:S(2)}) async-start(s16[4,208,1408]{2,1,0:T(8,128)(2,1)} %copy-done.7), calls=%async_computation.3 | async-start | bytes 4685824 | tf_op jit(solution)/shard_map/all_to_all | solution.py:277
  247.3 4.5 %decode.2.refs_0_ = f32[448,1344]{1,0:T(8,128)} custom-call(s32[1]{0:T(128)} %bitcast.odd_ref, s16[4,272,1408]{2,1,0:T(8,128)(2,1)} %all-to-all-done.2.refs_2_.rows.levels, s16[4,272,1408]{2,1,0:T(8,128)(2,1)} %all-to-all-done.2.refs_2_.rows.levels), custom_call_target="tpu_custom_call" | custom-call | flops 1 | bytes 1 | tf_op jit(solution)/shard_map/decode/pallas_call | solution.py:205
  251.8 24.1 %all-to-all-done.3.rows.levels = s16[4,208,1408]{2,1,0:T(8,128)(2,1)S(1)} async-done(((s16[4,208,1408]{2,1,0:T(8,128)(2,1)}), s16[4,208,1408]{2,1,0:T(8,128)(2,1)S(1)}, u32[]{:S(2)}, u32[]{:S(2)}) %all-to-all-start.3) | async-done | bytes 2342944 | tf_op jit(solution)/shard_map/all_to_all | solution.py:277
  276.0 2.4 decode.3
  (33 shorter events, 0.1 us)
Async XLA Ops:
  11.0 38.1 %all-to-all-start = ((bf16[16,128,512]{2,1,0:T(8,128)(2,1)}), bf16[16,128,512]{2,1,0:T(8,128)(2,1)S(1)}, u32[]{:S(2)}, u32[]{:S(2)}) async-start(bf16[16,128,512]{2,1,0:T(8,128)(2,1)} %cut_windows.2), calls=%async_computation | async-start | bytes 4194304 | tf_op jit(solution)/shard_map/all_to_all | solution.py:263
  18.6 137.1 %all-gather.7.cloned.1.call-start = ((), (), s32[]{:S(2)}) async-start(), calls=%async_computation.5 | async-start | bytes 8912896 | tf_op jit(solution)/shard_map/all_gather | solution.py:268
  22.6 14.0 %collective-permute-start = (bf16[20,3584]{1,0:T(8,128)(2,1)}, bf16[20,3584]{1,0:T(8,128)(2,1)S(1)}, u32[]{:S(2)}, u32[]{:S(2)}) collective-permute-start(bf16[20,3584]{1,0:T(8,128)(2,1)} %get-tuple-element.16), channel_id=1, source_target_pairs={{0,16},{16,0},{32,48},{48,32},{64,80},{80,64},{96,112},{112,96},{1... | collective-permute-start | bytes 430088 | tf_op jit(solution)/shard_map/ppermute | solution.py:243
  23.7 13.8 %collective-permute-start.1 = (bf16[20,3584]{1,0:T(8,128)(2,1)}, bf16[20,3584]{1,0:T(8,128)(2,1)S(1)}, u32[]{:S(2)}, u32[]{:S(2)}) collective-permute-start(bf16[20,3584]{1,0:T(8,128)(2,1)} %get-tuple-element.17), channel_id=1, source_target_pairs={{0,32},{16,48},{32,64},{48,80},{64,96},{80,112},{96,0},{112,16},{1... | collective-permute-start | bytes 430088 | tf_op jit(solution)/shard_map/ppermute | solution.py:243
  25.2 14.0 %collective-permute-start.2 = (bf16[20,3584]{1,0:T(8,128)(2,1)}, bf16[20,3584]{1,0:T(8,128)(2,1)S(1)}, u32[]{:S(2)}, u32[]{:S(2)}) collective-permute-start(bf16[20,3584]{1,0:T(8,128)(2,1)} %get-tuple-element.18), channel_id=1, source_target_pairs={{0,48},{16,32},{32,80},{48,64},{64,112},{80,96},{96,16},{112,0},{1... | collective-permute-start | bytes 430088 | tf_op jit(solution)/shard_map/ppermute | solution.py:243
  27.2 13.5 %collective-permute-start.3 = (bf16[20,3584]{1,0:T(8,128)(2,1)}, bf16[20,3584]{1,0:T(8,128)(2,1)S(1)}, u32[]{:S(2)}, u32[]{:S(2)}) collective-permute-start(bf16[20,3584]{1,0:T(8,128)(2,1)} %get-tuple-element.19), channel_id=1, source_target_pairs={{0,64},{16,80},{32,96},{48,112},{64,0},{80,16},{96,32},{112,48},{1... | collective-permute-start | bytes 430088 | tf_op jit(solution)/shard_map/ppermute | solution.py:243
  28.5 15.9 %collective-permute-start.4 = (bf16[20,3584]{1,0:T(8,128)(2,1)}, bf16[20,3584]{1,0:T(8,128)(2,1)S(1)}, u32[]{:S(2)}, u32[]{:S(2)}) collective-permute-start(bf16[20,3584]{1,0:T(8,128)(2,1)} %get-tuple-element.20), channel_id=1, source_target_pairs={{0,80},{16,64},{32,112},{48,96},{64,16},{80,0},{96,48},{112,32},{1... | collective-permute-start | bytes 430088 | tf_op jit(solution)/shard_map/ppermute | solution.py:243
  30.5 5.0 %copy-start.15 = (s32[32,1]{0,1:T(1,128)S(1)}, s32[32,1]{0,1:T(1,128)}, u32[]{:S(2)}) copy-start(s32[32,1]{0,1:T(1,128)} %param.6) | copy-start | bytes 388
  30.5 5.7 %copy-start.16 = (s32[1,4]{1,0:T(1,128)S(1)}, s32[1,4]{1,0:T(1,128)}, u32[]{:S(2)}) copy-start(s32[1,4]{1,0:T(1,128)} %param.5) | copy-start | bytes 52
  30.5 7.0 %copy-start.17 = (bf16[20,3584]{1,0:T(8,128)(2,1)S(1)}, bf16[20,3584]{1,0:T(8,128)(2,1)}, u32[]{:S(2)}) copy-start(bf16[20,3584]{1,0:T(8,128)(2,1)} %get-tuple-element.22) | copy-start | bytes 430084
  36.6 12.5 %copy-start.8 = (bf16[20,3584]{1,0:T(8,128)(2,1)}, bf16[20,3584]{1,0:T(8,128)(2,1)S(1)}, u32[]{:S(2)}) copy-start(bf16[20,3584]{1,0:T(8,128)(2,1)S(1)} %collective-permute-done.refs_1_) | copy-start | bytes 430084
  36.6 7.8 %collective-permute-start.5 = (bf16[20,3584]{1,0:T(8,128)(2,1)}, bf16[20,3584]{1,0:T(8,128)(2,1)S(1)}, u32[]{:S(2)}, u32[]{:S(2)}) collective-permute-start(bf16[20,3584]{1,0:T(8,128)(2,1)} %get-tuple-element.21), channel_id=1, source_target_pairs={{0,96},{16,112},{32,0},{48,16},{64,32},{80,48},{96,64},{112,80},{1... | collective-permute-start | bytes 430088 | tf_op jit(solution)/shard_map/ppermute | solution.py:243
  37.5 11.5 %copy-start.9 = (bf16[20,3584]{1,0:T(8,128)(2,1)}, bf16[20,3584]{1,0:T(8,128)(2,1)S(1)}, u32[]{:S(2)}) copy-start(bf16[20,3584]{1,0:T(8,128)(2,1)S(1)} %collective-permute-done.1.refs_2_) | copy-start | bytes 430084
  37.5 9.1 %collective-permute-start.6 = (bf16[20,3584]{1,0:T(8,128)(2,1)S(1)}, bf16[20,3584]{1,0:T(8,128)(2,1)S(1)}, u32[]{:S(2)}, u32[]{:S(2)}) collective-permute-start(bf16[20,3584]{1,0:T(8,128)(2,1)S(1)} %copy-done.17), channel_id=1, source_target_pairs={{0,112},{16,96},{32,16},{48,0},{64,48},{80,32},{96,80},{112,64},{1... | collective-permute-start | bytes 430088 | tf_op jit(solution)/shard_map/ppermute | solution.py:243
  39.1 9.9 %copy-start.10 = (bf16[20,3584]{1,0:T(8,128)(2,1)}, bf16[20,3584]{1,0:T(8,128)(2,1)S(1)}, u32[]{:S(2)}) copy-start(bf16[20,3584]{1,0:T(8,128)(2,1)S(1)} %collective-permute-done.2.refs_3_) | copy-start | bytes 430084
  40.6 8.4 %copy-start.11 = (bf16[20,3584]{1,0:T(8,128)(2,1)}, bf16[20,3584]{1,0:T(8,128)(2,1)S(1)}, u32[]{:S(2)}) copy-start(bf16[20,3584]{1,0:T(8,128)(2,1)S(1)} %collective-permute-done.3.refs_4_) | copy-start | bytes 430084
  44.4 4.7 %copy-start.12 = (bf16[20,3584]{1,0:T(8,128)(2,1)}, bf16[20,3584]{1,0:T(8,128)(2,1)S(1)}, u32[]{:S(2)}) copy-start(bf16[20,3584]{1,0:T(8,128)(2,1)S(1)} %collective-permute-done.4.refs_5_) | copy-start | bytes 430084
  44.4 4.7 %copy-start.13 = (bf16[20,3584]{1,0:T(8,128)(2,1)}, bf16[20,3584]{1,0:T(8,128)(2,1)S(1)}, u32[]{:S(2)}) copy-start(bf16[20,3584]{1,0:T(8,128)(2,1)S(1)} %collective-permute-done.5.refs_6_) | copy-start | bytes 430084
  46.6 2.4 copy-start.14
  49.0 1.3 copy-start.2
  54.5 164.3 %all-gather.5.cloned.1.call-start = ((), (), s32[]{:S(2)}) async-start(), calls=%async_computation.4 | async-start | bytes 6684672 | tf_op jit(solution)/shard_map/all_gather | solution.py:268
  55.2 100.4 %copy-start.3 = (bf16[16,128,512]{2,1,0:T(8,128)(2,1)S(1)}, bf16[16,128,512]{2,1,0:T(8,128)(2,1)}, u32[]{:S(2)}) copy-start(bf16[16,128,512]{2,1,0:T(8,128)(2,1)} %copy-done.2) | copy-start | bytes 6291460
  155.6 2.0 copy-start
  157.7 3.4 %copy-start.4 = (bf16[32768,128]{1,0:T(8,128)(2,1)S(1)}, bf16[32768,128]{1,0:T(8,128)(2,1)}, u32[]{:S(2)}) copy-start(bf16[32768,128]{1,0:T(8,128)(2,1)} %all-gather.7.cloned.1.call-done) | copy-start | bytes 25165828
  168.2 9.8 %collective-permute-start.7 = (f32[1024,1408]{1,0:T(8,128)S(1)}, f32[1024,1408]{1,0:T(8,128)S(1)}, u32[]{:S(2)}, u32[]{:S(2)}) collective-permute-start(f32[1024,1408]{1,0:T(8,128)S(1)} %multiply.4.refs_2_), channel_id=1, source_target_pairs={{0,16},{16,0},{32,48},{48,32},{64,80},{80,64},{96,112},{112,96},{1... | collective-permute-start | bytes 17301512 | tf_op jit(solution)/shard_map/ppermute | solution.py:275
  179.6 1.6 copy-start.6
  181.2 41.2 %all-to-all-start.2 = ((s16[4,272,1408]{2,1,0:T(8,128)(2,1)}), s16[4,272,1408]{2,1,0:T(8,128)(2,1)}, u32[]{:S(2)}, u32[]{:S(2)}) async-start(s16[4,272,1408]{2,1,0:T(8,128)(2,1)} %copy-done.6), calls=%async_computation.2 | async-start | bytes 6127616 | tf_op jit(solution)/shard_map/all_to_all | solution.py:277
  222.3 2.0 copy-start.1
  224.4 2.8 copy-start.5
  232.6 8.4 %collective-permute-start.8 = (f32[768,1408]{1,0:T(8,128)S(1)}, f32[768,1408]{1,0:T(8,128)S(1)}, u32[]{:S(2)}, u32[]{:S(2)}) collective-permute-start(f32[768,1408]{1,0:T(8,128)S(1)} %multiply.6.refs_2_), channel_id=1, source_target_pairs={{0,16},{16,0},{32,48},{48,32},{64,80},{80,64},{96,112},{112,96},{1... | collective-permute-start | bytes 12976136 | tf_op jit(solution)/shard_map/ppermute | solution.py:275
  242.2 1.4 copy-start.7
  243.6 32.3 %all-to-all-start.3 = ((s16[4,208,1408]{2,1,0:T(8,128)(2,1)}), s16[4,208,1408]{2,1,0:T(8,128)(2,1)S(1)}, u32[]{:S(2)}, u32[]{:S(2)}) async-start(s16[4,208,1408]{2,1,0:T(8,128)(2,1)} %copy-done.7), calls=%async_computation.3 | async-start | bytes 4685824 | tf_op jit(solution)/shard_map/all_to_all | solution.py:277
Sparse Core Ops, SparseCore 0:
  54.6 100.9 all-gather.6
  157.8 60.9 all-gather.4

commit v5 on v4

--- a/solution.py
+++ b/solution.py
@@ -69,13 +69,14 @@
     block = rows // count
 
     def kernel(targets_ref, cot_ref, *out_refs):
-        row = lax.broadcasted_iota(jnp.int32, (block, rows), 0)
-        column = lax.broadcasted_iota(jnp.int32, (block, rows), 1)
-        for j in range(count):
-            taking = (column == row + targets_ref[j] * block).astype(jnp.bfloat16)
-            out_refs[j][...] = jnp.dot(
-                taking, cot_ref[...], preferred_element_type=jnp.float32
-            ).astype(jnp.bfloat16)
+        row = lax.broadcasted_iota(jnp.int32, (PLACE, rows), 0)
+        column = lax.broadcasted_iota(jnp.int32, (PLACE, rows), 1)
+        taking = jnp.concatenate(
+            [(column == row + targets_ref[j] * block).astype(jnp.bfloat16) for j in range(count)]
+        )
+        taken = jnp.dot(taking, cot_ref[...], preferred_element_type=jnp.float32)
+        for j, out_ref in enumerate(out_refs):
+            out_ref[...] = taken[j * PLACE : j * PLACE + block].astype(jnp.bfloat16)
 
     return pl.pallas_call(
         kernel,
@@ -136,7 +137,7 @@
 def multiply(cot, features, core, *awaited):
     source_count, rows, tok_count = cot.shape
     width = sum(f.shape[2] for f in features)
-    steps = 2
+    steps = 1
     tile = rows // (2 * steps)
 
     def kernel(cot_ref, *refs):

time: 286 us -> 285 us (level)
  transfers between devices with their start and end apart: 14 -> 14, of which waited for: 10 -> 10; matrix products, arithmetic and copies ran while one was open for 1% -> 1% of each run, Pallas kernels for 12% -> 11%
where the time goes in v5:
time: 285 us; the launch traced here: 284 us
  waiting for transfers between devices  119 us (42%)
  blocking collectives  56.9 us (20%)
  Pallas kernels  49.7 us (17%)
  starting transfers between devices  27.9 us (10%)
  local copies, waits for them, and re-layouts  15.7 us (6%)
  between operations  13.7 us (5%)
    all_gather x2, waiting for transfers between devices, body(): lax.all_gather(cot, 'dev', axis=0, tiled=False)  76.6 us
    all_to_all x1, blocking collectives, exchange(): return lax.all_to_all(cut, 'dev', split_axis=0, concat_axis=0, tiled=True)  56.9 us
    all_to_all x2, waiting for transfers between devices, body(): lax.all_to_all(code(own, got), 'role', split_axis=0, concat_axis=0, axis_...  27.4 us
    pallas_call x4, Pallas kernels, multiply(): pl.pallas_call(kernel, grid=(steps,), in_specs=[pl.BlockSpec((source_coun...  23.5 us
    unnamed x36, local copies, waits for them, and re-layouts  14.6 us
    ppermute x7, starting transfers between devices, body(): lax.ppermute(block, 'role', along_z(*step))  9.85 us
    pallas_call x2, Pallas kernels, cut_windows(): pl.pallas_call(kernel, grid=(tok_count // tile,), in_specs=[pl.BlockSpec(...  9.38 us
    all_to_all x2, starting transfers between devices, body(): lax.all_to_all(code(own, got), 'role', split_axis=0, concat_axis=0, axis_...  8.46 us
  transfers between devices with their start and end apart: 14, of which 10 were waited for; matrix products, arithmetic and copies ran while one was open for 1% of the time, Pallas kernels for 11%

profile of v5, /device:TPU:1, one launch (start us, length us, event | category | flops | bytes accessed | tf_op | source)
XLA Modules:
  0.0 284.3 jit_solution(6833686495543124078)
XLA Ops:
  6.5 4.4 %cut_windows.2 = bf16[16,128,512]{2,1,0:T(8,128)(2,1)} custom-call(bf16[128,21504]{1,0:T(8,128)(2,1)} %rows_ref.3), custom_call_target="tpu_custom_call" | custom-call | tf_op jit(solution)/shard_map/cut_windows/pallas_call | solution.py:39
  11.0 7.6 %all-to-all-start = ((bf16[16,128,512]{2,1,0:T(8,128)(2,1)}), bf16[16,128,512]{2,1,0:T(8,128)(2,1)S(1)}, u32[]{:S(2)}, u32[]{:S(2)}) async-start(bf16[16,128,512]{2,1,0:T(8,128)(2,1)} %cut_windows.2), calls=%async_computation | async-start | bytes 4194304 | tf_op jit(solution)/shard_map/all_to_all | solution.py:264
  18.6 0.0 all-gather.7.cloned.1.call-start
  18.7 0.6 stack.65.targets_ref
  19.3 2.9 %sort_blocks.1 = (bf16[20,3584]{1,0:T(8,128)(2,1)}, bf16[20,3584]{1,0:T(8,128)(2,1)}, bf16[20,3584]{1,0:T(8,128)(2,1)}, bf16[20,3584]{1,0:T(8,128)(2,1)}, bf16[2...) custom-call(s32[8]{0:T(128)} %stack.65.targets_ref, ...), custom_call_target="tpu_custom_call" | custom-call | tf_op jit(solution)/shard_map/sort_blocks/pallas_call | solution.py:81
  22.2 0.9 collective-permute-start
  23.2 1.6 collective-permute-start.1
  24.8 1.8 collective-permute-start.2
  26.6 1.5 collective-permute-start.3
  28.1 1.9 collective-permute-start.4
  30.0 5.0 %cut_windows.3.refs_9_.value_ref = bf16[16,128,896]{2,1,0:T(8,128)(2,1)} custom-call(bf16[128,21504]{1,0:T(8,128)(2,1)} %rows_ref.3), custom_call_target="tpu_custom_call" | custom-call | tf_op jit(solution)/shard_map/cut_windows/pallas_call | solution.py:39
  35.0 0.1 broadcast_in_dim.6
  35.0 0.1 eq.91
  35.1 0.1 fusion
  35.2 0.1 reduce_window_sum.11
  35.3 0.2 select_reduce_fusion
  35.5 0.1 broadcast_in_dim.7
  35.5 0.1 mul.56
  35.7 0.1 broadcast_in_dim.16
  35.7 0.1 reshape.99
  35.8 0.1 stack.58
  35.9 0.1 broadcast_compare_fusion
  36.0 0.0 collective-permute-done.refs_1_
  36.0 1.1 collective-permute-start.5
  37.1 0.0 collective-permute-done.1.refs_2_
  37.1 1.0 collective-permute-start.6
  38.1 0.6 and_convert_fusion.places_ref
  38.8 0.0 collective-permute-done.2.refs_3_
  38.8 1.5 collective-permute-done.3.refs_4_
  40.3 3.8 %collective-permute-done.4.refs_5_ = bf16[20,3584]{1,0:T(8,128)(2,1)S(1)} collective-permute-done((bf16[20,3584]{1,0:T(8,128)(2,1)}, bf16[20,3584]{1,0:T(8,128)(2,1)S(1)}, u32[]{:S(2)}, u32[]{:S(2)}) %collective-permute-start.4) | collective-permute-done | bytes 143392 | tf_op jit(solution)/shard_map/ppermute | solution.py:244
  44.0 0.0 collective-permute-done.5.refs_6_
  44.0 2.3 collective-permute-done.6.refs_7_
  46.4 2.6 all-to-all-done.refs_8_.refs_0_
  49.1 1.3 copy-done.2
  50.4 4.1 %pair_rows.1 = (bf16[2048,128]{1,0:T(8,128)(2,1)}, bf16[1536,128]{1,0:T(8,128)(2,1)}) custom-call(s32[1]{0:T(128)} %bitcast.1.core_ref, bf16[8,32,128]{2,1,0:T(8,128)(2,1)} %and_convert_fusion.places_ref, bf16[20,3584]{1,0:T(8,128)(2,1)} %get-tuple-element.15.refs_0_, bf16[20,3584]{1,0:T(8,128)(2,1)} %copy-done.8, bf16[20,3584]{1,0:T(8,128)(2,1)} %copy-done.9, ...), custom_call_target="tpu_custom_call" | custom-call | tf_op jit(solution)/shard_map/pair_rows/pallas_call | solution.py:123
  54.4 0.0 all-gather.7.cloned.1.call-update
  54.5 0.0 all-gather.5.cloned.1.call-start
  54.5 0.7 all-gather.5.cloned.1.call-update
  55.2 0.0 copy-start.3
  55.2 56.9 %all_to_all.20.refs_1_ = bf16[16,128,896]{2,1,0:T(8,128)(2,1)} all-to-all(bf16[16,128,896]{2,1,0:T(8,128)(2,1)} %hold.1), channel_id=1, replica_groups=mesh['role'=8,'dev'=16] {'dev'}, dimensions={0} | all-to-all | bytes 7340032 | tf_op jit(solution)/shard_map/all_to_all | solution.py:264
  112.2 43.4 %all-gather.7.cloned.1.call-done = bf16[32768,128]{1,0:T(8,128)(2,1)} async-done(((bf16[2048,128]{1,0:T(8,128)(2,1)}), bf16[32768,128]{1,0:T(8,128)(2,1)}) %all-gather.7.cloned.1.call-update) | async-done | bytes 8388624 | tf_op jit(solution)/shard_map/all_gather | solution.py:269
  155.6 2.0 copy-done
  157.7 3.4 %copy-done.4 = bf16[32768,128]{1,0:T(8,128)(2,1)S(1)} copy-done((bf16[32768,128]{1,0:T(8,128)(2,1)S(1)}, bf16[32768,128]{1,0:T(8,128)(2,1)}, u32[]{:S(2)}) %copy-start.4) | copy-done | bytes 8388632
  161.0 6.7 %multiply.4.refs_2_ = f32[1024,1408]{1,0:T(8,128)S(1)} custom-call(bf16[16,2048,128]{2,1,0:T(8,128)(2,1)S(1)} %bitcast.20, bf16[16,128,512]{2,1,0:T(8,128)(2,1)S(1)} %copy-done.3, bf16[16,128,896]{2,1,0:T(8,128)(2,1)S(1)} %copy-done), custom_call_target="tpu_custom_call" | custom-call | flops 1 | bytes 1 | tf_op jit(solution)/shard_map/multiply/pallas_call | solution.py:153
  167.7 0.8 collective-permute-start.7
  168.5 6.7 %multiply.5.own_ref = f32[1024,1408]{1,0:T(8,128)S(1)} custom-call(bf16[16,2048,128]{2,1,0:T(8,128)(2,1)S(1)} %bitcast.21, bf16[16,128,512]{2,1,0:T(8,128)(2,1)S(1)} %copy-done.3, bf16[16,128,896]{2,1,0:T(8,128)(2,1)S(1)} %copy-done, f32[1024,1408]{1,0:T(8,128)S(1)} %multiply.4.refs_2_), custom_call_target="tpu_custom_call" | custom-call | flops 1 | bytes 1 | tf_op jit(solution)/shard_map/multiply/pallas_call | solution.py:153
  175.2 2.3 collective-permute-done.7.got_ref
  177.5 1.6 code.2
  179.2 1.6 copy-done.6
  180.7 4.8 %all-to-all-start.2 = ((s16[4,272,1408]{2,1,0:T(8,128)(2,1)}), s16[4,272,1408]{2,1,0:T(8,128)(2,1)}, u32[]{:S(2)}, u32[]{:S(2)}) async-start(s16[4,272,1408]{2,1,0:T(8,128)(2,1)} %copy-done.6), calls=%async_computation.2 | async-start | bytes 6127616 | tf_op jit(solution)/shard_map/all_to_all | solution.py:278
  185.6 33.1 %all-gather.5.cloned.1.call-done = bf16[24576,128]{1,0:T(8,128)(2,1)} async-done(((bf16[1536,128]{1,0:T(8,128)(2,1)}), bf16[24576,128]{1,0:T(8,128)(2,1)}) %all-gather.5.cloned.1.call-update) | async-done | bytes 6291472 | tf_op jit(solution)/shard_map/all_gather | solution.py:269
  218.7 3.3 %all-to-all-done.2.refs_2_.rows.levels = s16[4,272,1408]{2,1,0:T(8,128)(2,1)} async-done(((s16[4,272,1408]{2,1,0:T(8,128)(2,1)}), s16[4,272,1408]{2,1,0:T(8,128)(2,1)}, u32[]{:S(2)}, u32[]{:S(2)}) %all-to-all-start.2) | async-done | bytes 3063840 | tf_op jit(solution)/shard_map/all_to_all | solution.py:278
  222.0 2.0 copy-done.1
  224.1 2.8 copy-done.5
  226.9 5.1 %multiply.6.refs_2_ = f32[768,1408]{1,0:T(8,128)S(1)} custom-call(bf16[16,1536,128]{2,1,0:T(8,128)(2,1)S(1)} %bitcast.22, bf16[16,128,512]{2,1,0:T(8,128)(2,1)S(1)} %copy-done.3, bf16[16,128,896]{2,1,0:T(8,128)(2,1)S(1)} %copy-done.1, s16[4,272,1408]{2,1,0:T(8,128)(2,1)} %all-to-all-done.2.refs_2_.rows.levels), custom_call_target="tpu_custom_call" | custom-call | flops 1 | bytes 1 | tf_op jit(solution)/shard_map/multiply/pallas_call | solution.py:153
  231.9 1.2 collective-permute-start.8
  233.2 5.1 %multiply.7.own_ref = f32[768,1408]{1,0:T(8,128)S(1)} custom-call(bf16[16,1536,128]{2,1,0:T(8,128)(2,1)S(1)} %bitcast.23, bf16[16,128,512]{2,1,0:T(8,128)(2,1)S(1)} %copy-done.3, bf16[16,128,896]{2,1,0:T(8,128)(2,1)S(1)} %copy-done.1, f32[768,1408]{1,0:T(8,128)S(1)} %multiply.6.refs_2_), custom_call_target="tpu_custom_call" | custom-call | flops 1 | bytes 1 | tf_op jit(solution)/shard_map/multiply/pallas_call | solution.py:153
  238.2 1.9 collective-permute-done.8.got_ref
  240.1 1.2 code.3
  241.4 1.4 copy-done.7
  242.8 3.6 %all-to-all-start.3 = ((s16[4,208,1408]{2,1,0:T(8,128)(2,1)}), s16[4,208,1408]{2,1,0:T(8,128)(2,1)S(1)}, u32[]{:S(2)}, u32[]{:S(2)}) async-start(s16[4,208,1408]{2,1,0:T(8,128)(2,1)} %copy-done.7), calls=%async_computation.3 | async-start | bytes 4685824 | tf_op jit(solution)/shard_map/all_to_all | solution.py:278
  246.4 4.5 %decode.2.refs_0_ = f32[448,1344]{1,0:T(8,128)} custom-call(s32[1]{0:T(128)} %bitcast.odd_ref, s16[4,272,1408]{2,1,0:T(8,128)(2,1)} %all-to-all-done.2.refs_2_.rows.levels, s16[4,272,1408]{2,1,0:T(8,128)(2,1)} %all-to-all-done.2.refs_2_.rows.levels), custom_call_target="tpu_custom_call" | custom-call | flops 1 | bytes 1 | tf_op jit(solution)/shard_map/decode/pallas_call | solution.py:206
  251.0 24.1 %all-to-all-done.3.rows.levels = s16[4,208,1408]{2,1,0:T(8,128)(2,1)S(1)} async-done(((s16[4,208,1408]{2,1,0:T(8,128)(2,1)}), s16[4,208,1408]{2,1,0:T(8,128)(2,1)S(1)}, u32[]{:S(2)}, u32[]{:S(2)}) %all-to-all-start.3) | async-done | bytes 2342944 | tf_op jit(solution)/shard_map/all_to_all | solution.py:278
  275.1 2.4 decode.3
  (33 shorter events, 0.1 us)
Async XLA Ops:
  11.0 38.1 %all-to-all-start = ((bf16[16,128,512]{2,1,0:T(8,128)(2,1)}), bf16[16,128,512]{2,1,0:T(8,128)(2,1)S(1)}, u32[]{:S(2)}, u32[]{:S(2)}) async-start(bf16[16,128,512]{2,1,0:T(8,128)(2,1)} %cut_windows.2), calls=%async_computation | async-start | bytes 4194304 | tf_op jit(solution)/shard_map/all_to_all | solution.py:264
  18.6 137.1 %all-gather.7.cloned.1.call-start = ((), (), s32[]{:S(2)}) async-start(), calls=%async_computation.5 | async-start | bytes 8912896 | tf_op jit(solution)/shard_map/all_gather | solution.py:269
  22.2 13.8 %collective-permute-start = (bf16[20,3584]{1,0:T(8,128)(2,1)}, bf16[20,3584]{1,0:T(8,128)(2,1)S(1)}, u32[]{:S(2)}, u32[]{:S(2)}) collective-permute-start(bf16[20,3584]{1,0:T(8,128)(2,1)} %get-tuple-element.16), channel_id=1, source_target_pairs={{0,16},{16,0},{32,48},{48,32},{64,80},{80,64},{96,112},{112,96},{1... | collective-permute-start | bytes 430088 | tf_op jit(solution)/shard_map/ppermute | solution.py:244
  23.2 14.0 %collective-permute-start.1 = (bf16[20,3584]{1,0:T(8,128)(2,1)}, bf16[20,3584]{1,0:T(8,128)(2,1)S(1)}, u32[]{:S(2)}, u32[]{:S(2)}) collective-permute-start(bf16[20,3584]{1,0:T(8,128)(2,1)} %get-tuple-element.17), channel_id=1, source_target_pairs={{0,32},{16,48},{32,64},{48,80},{64,96},{80,112},{96,0},{112,16},{1... | collective-permute-start | bytes 430088 | tf_op jit(solution)/shard_map/ppermute | solution.py:244
  24.8 13.9 %collective-permute-start.2 = (bf16[20,3584]{1,0:T(8,128)(2,1)}, bf16[20,3584]{1,0:T(8,128)(2,1)S(1)}, u32[]{:S(2)}, u32[]{:S(2)}) collective-permute-start(bf16[20,3584]{1,0:T(8,128)(2,1)} %get-tuple-element.18), channel_id=1, source_target_pairs={{0,48},{16,32},{32,80},{48,64},{64,112},{80,96},{96,16},{112,0},{1... | collective-permute-start | bytes 430088 | tf_op jit(solution)/shard_map/ppermute | solution.py:244
  26.6 13.6 %collective-permute-start.3 = (bf16[20,3584]{1,0:T(8,128)(2,1)}, bf16[20,3584]{1,0:T(8,128)(2,1)S(1)}, u32[]{:S(2)}, u32[]{:S(2)}) collective-permute-start(bf16[20,3584]{1,0:T(8,128)(2,1)} %get-tuple-element.19), channel_id=1, source_target_pairs={{0,64},{16,80},{32,96},{48,112},{64,0},{80,16},{96,32},{112,48},{1... | collective-permute-start | bytes 430088 | tf_op jit(solution)/shard_map/ppermute | solution.py:244
  28.1 15.9 %collective-permute-start.4 = (bf16[20,3584]{1,0:T(8,128)(2,1)}, bf16[20,3584]{1,0:T(8,128)(2,1)S(1)}, u32[]{:S(2)}, u32[]{:S(2)}) collective-permute-start(bf16[20,3584]{1,0:T(8,128)(2,1)} %get-tuple-element.20), channel_id=1, source_target_pairs={{0,80},{16,64},{32,112},{48,96},{64,16},{80,0},{96,48},{112,32},{1... | collective-permute-start | bytes 430088 | tf_op jit(solution)/shard_map/ppermute | solution.py:244
  30.0 5.0 %copy-start.15 = (s32[32,1]{0,1:T(1,128)S(1)}, s32[32,1]{0,1:T(1,128)}, u32[]{:S(2)}) copy-start(s32[32,1]{0,1:T(1,128)} %param.6) | copy-start | bytes 388
  30.0 5.7 %copy-start.16 = (s32[1,4]{1,0:T(1,128)S(1)}, s32[1,4]{1,0:T(1,128)}, u32[]{:S(2)}) copy-start(s32[1,4]{1,0:T(1,128)} %param.5) | copy-start | bytes 52
  30.0 7.2 %copy-start.17 = (bf16[20,3584]{1,0:T(8,128)(2,1)S(1)}, bf16[20,3584]{1,0:T(8,128)(2,1)}, u32[]{:S(2)}) copy-start(bf16[20,3584]{1,0:T(8,128)(2,1)} %get-tuple-element.22) | copy-start | bytes 430084
  36.0 13.0 %copy-start.8 = (bf16[20,3584]{1,0:T(8,128)(2,1)}, bf16[20,3584]{1,0:T(8,128)(2,1)S(1)}, u32[]{:S(2)}) copy-start(bf16[20,3584]{1,0:T(8,128)(2,1)S(1)} %collective-permute-done.refs_1_) | copy-start | bytes 430084
  36.0 8.0 %collective-permute-start.5 = (bf16[20,3584]{1,0:T(8,128)(2,1)}, bf16[20,3584]{1,0:T(8,128)(2,1)S(1)}, u32[]{:S(2)}, u32[]{:S(2)}) collective-permute-start(bf16[20,3584]{1,0:T(8,128)(2,1)} %get-tuple-element.21), channel_id=1, source_target_pairs={{0,96},{16,112},{32,0},{48,16},{64,32},{80,48},{96,64},{112,80},{1... | collective-permute-start | bytes 430088 | tf_op jit(solution)/shard_map/ppermute | solution.py:244
  37.1 11.9 %copy-start.9 = (bf16[20,3584]{1,0:T(8,128)(2,1)}, bf16[20,3584]{1,0:T(8,128)(2,1)S(1)}, u32[]{:S(2)}) copy-start(bf16[20,3584]{1,0:T(8,128)(2,1)S(1)} %collective-permute-done.1.refs_2_) | copy-start | bytes 430084
  37.1 9.2 %collective-permute-start.6 = (bf16[20,3584]{1,0:T(8,128)(2,1)S(1)}, bf16[20,3584]{1,0:T(8,128)(2,1)S(1)}, u32[]{:S(2)}, u32[]{:S(2)}) collective-permute-start(bf16[20,3584]{1,0:T(8,128)(2,1)S(1)} %copy-done.17), channel_id=1, source_target_pairs={{0,112},{16,96},{32,16},{48,0},{64,48},{80,32},{96,80},{112,64},{1... | collective-permute-start | bytes 430088 | tf_op jit(solution)/shard_map/ppermute | solution.py:244
  38.8 10.3 %copy-start.10 = (bf16[20,3584]{1,0:T(8,128)(2,1)}, bf16[20,3584]{1,0:T(8,128)(2,1)S(1)}, u32[]{:S(2)}) copy-start(bf16[20,3584]{1,0:T(8,128)(2,1)S(1)} %collective-permute-done.2.refs_3_) | copy-start | bytes 430084
  40.3 8.8 %copy-start.11 = (bf16[20,3584]{1,0:T(8,128)(2,1)}, bf16[20,3584]{1,0:T(8,128)(2,1)S(1)}, u32[]{:S(2)}) copy-start(bf16[20,3584]{1,0:T(8,128)(2,1)S(1)} %collective-permute-done.3.refs_4_) | copy-start | bytes 430084
  44.0 5.0 %copy-start.12 = (bf16[20,3584]{1,0:T(8,128)(2,1)}, bf16[20,3584]{1,0:T(8,128)(2,1)S(1)}, u32[]{:S(2)}) copy-start(bf16[20,3584]{1,0:T(8,128)(2,1)S(1)} %collective-permute-done.4.refs_5_) | copy-start | bytes 430084
  44.0 5.0 %copy-start.13 = (bf16[20,3584]{1,0:T(8,128)(2,1)}, bf16[20,3584]{1,0:T(8,128)(2,1)S(1)}, u32[]{:S(2)}) copy-start(bf16[20,3584]{1,0:T(8,128)(2,1)S(1)} %collective-permute-done.5.refs_6_) | copy-start | bytes 430084
  46.4 2.7 copy-start.14
  49.0 1.3 copy-start.2
  54.5 164.3 %all-gather.5.cloned.1.call-start = ((), (), s32[]{:S(2)}) async-start(), calls=%async_computation.4 | async-start | bytes 6684672 | tf_op jit(solution)/shard_map/all_gather | solution.py:269
  55.2 100.4 %copy-start.3 = (bf16[16,128,512]{2,1,0:T(8,128)(2,1)S(1)}, bf16[16,128,512]{2,1,0:T(8,128)(2,1)}, u32[]{:S(2)}) copy-start(bf16[16,128,512]{2,1,0:T(8,128)(2,1)} %copy-done.2) | copy-start | bytes 6291460
  155.6 2.0 copy-start
  157.7 3.4 %copy-start.4 = (bf16[32768,128]{1,0:T(8,128)(2,1)S(1)}, bf16[32768,128]{1,0:T(8,128)(2,1)}, u32[]{:S(2)}) copy-start(bf16[32768,128]{1,0:T(8,128)(2,1)} %all-gather.7.cloned.1.call-done) | copy-start | bytes 25165828
  167.7 9.8 %collective-permute-start.7 = (f32[1024,1408]{1,0:T(8,128)S(1)}, f32[1024,1408]{1,0:T(8,128)S(1)}, u32[]{:S(2)}, u32[]{:S(2)}) collective-permute-start(f32[1024,1408]{1,0:T(8,128)S(1)} %multiply.4.refs_2_), channel_id=1, source_target_pairs={{0,16},{16,0},{32,48},{48,32},{64,80},{80,64},{96,112},{112,96},{1... | collective-permute-start | bytes 17301512 | tf_op jit(solution)/shard_map/ppermute | solution.py:276
  179.1 1.6 copy-start.6
  180.7 41.3 %all-to-all-start.2 = ((s16[4,272,1408]{2,1,0:T(8,128)(2,1)}), s16[4,272,1408]{2,1,0:T(8,128)(2,1)}, u32[]{:S(2)}, u32[]{:S(2)}) async-start(s16[4,272,1408]{2,1,0:T(8,128)(2,1)} %copy-done.6), calls=%async_computation.2 | async-start | bytes 6127616 | tf_op jit(solution)/shard_map/all_to_all | solution.py:278
  222.0 2.0 copy-start.1
  224.1 2.8 copy-start.5
  231.9 8.2 %collective-permute-start.8 = (f32[768,1408]{1,0:T(8,128)S(1)}, f32[768,1408]{1,0:T(8,128)S(1)}, u32[]{:S(2)}, u32[]{:S(2)}) collective-permute-start(f32[768,1408]{1,0:T(8,128)S(1)} %multiply.6.refs_2_), channel_id=1, source_target_pairs={{0,16},{16,0},{32,48},{48,32},{64,80},{80,64},{96,112},{112,96},{1... | collective-permute-start | bytes 12976136 | tf_op jit(solution)/shard_map/ppermute | solution.py:276
  241.3 1.4 copy-start.7
  242.8 32.3 %all-to-all-start.3 = ((s16[4,208,1408]{2,1,0:T(8,128)(2,1)}), s16[4,208,1408]{2,1,0:T(8,128)(2,1)S(1)}, u32[]{:S(2)}, u32[]{:S(2)}) async-start(s16[4,208,1408]{2,1,0:T(8,128)(2,1)} %copy-done.7), calls=%async_computation.3 | async-start | bytes 4685824 | tf_op jit(solution)/shard_map/all_to_all | solution.py:278
Sparse Core Ops, SparseCore 0:
  54.6 100.9 all-gather.6
  157.8 60.9 all-gather.4
